TPU v7x, 256 devices: a whole 4x4x8 slice. The times are simulated.
256 devices in a mesh: dp: 4 (over y), row: 4 (over x), col: 16 (over z, core).
Axes of the slice: x: 4, y: 4, z: 8, core: 2. Of those that a mesh axis runs over, the one named last changes fastest.
Arguments:
- tokens_in: bfloat16 [1024, 12288], P(('dp', 'col'), 'row'), may hold values from -28 to 28
- out_grad: bfloat16 [1024, 49152], P('dp', 'col'), may hold values from -8 to 8
- row_state: float32 [12288], P('row'), as said below
- col_state: float32 [49152], P(('col', 'dp')), as said below
Outputs:
- update: float32 [12288, 49152], P('row', ('col', 'dp'))
- row_stats: float32 [12288], P('row')
- col_stats: float32 [49152], P(('col', 'dp'))
Inputs may be any that keep to these rules, and one draw needn't show every extreme that they name: `row_state`: positive. `col_state`: positive.
All inputs are finite; a program needn't handle non-finite values.
Results may differ from a plain program's by a relative error of at most 0.0003.
Values may be sent and summed in bfloat16 or wider, within the bound.
No kernel may reach another device: no remote copies, remote signals or barrier semaphores. Data moves between devices by JAX's collectives and lax.ppermute only.
A program may use at most 64 MiB of HBM per device.

v0:
```python
import jax
import jax.numpy as jnp
from jax import lax
from jax.sharding import PartitionSpec as P

D = 12288
F = 49152


DECAY = 0.7
CLIP = 1.0


def on_device(tokens_in, out_grad, row_state, col_state):
    grad_cols = lax.all_to_all(out_grad, "dp", split_axis=1, concat_axis=0, tiled=True)
    group_tokens = lax.all_gather(tokens_in, "col", axis=0, tiled=True)
    weight_grad = lax.dot_general(
        lax.all_gather(group_tokens, "dp", axis=0, tiled=True),
        grad_cols,
        (((0,), (0,)), ((), ())),
        preferred_element_type=jnp.float32,
    )
    squared = weight_grad * weight_grad
    row_sum = lax.psum(jnp.sum(squared, axis=1), ("dp", "col"))
    col_part = jnp.sum(squared, axis=0)
    row_stats = DECAY * row_state + (1.0 - DECAY) * (row_sum / F)
    col_sum, row_total = lax.psum((col_part, jnp.sum(row_stats)), "row")
    col_stats = DECAY * col_state + (1.0 - DECAY) * (col_sum / D)
    row_mean = row_total / D
    raw_update = (
        weight_grad * lax.rsqrt(row_stats / row_mean)[:, None] * lax.rsqrt(col_stats)[None, :]
    )
    power_sum = lax.psum(jnp.sum(raw_update * raw_update), ("dp", "row", "col"))
    clip_factor = jnp.maximum(1.0, jnp.sqrt(power_sum / (D * F)) / CLIP)
    return (raw_update / clip_factor, row_stats, col_stats)


def solution(mesh):
    return jax.shard_map(
        on_device,
        mesh=mesh,
        in_specs=(P(("dp", "col"), "row"), P("dp", "col"), P("row"), P(("col", "dp"))),
        out_specs=(P("row", ("col", "dp")), P("row"), P(("col", "dp"))),
        check_vma=False,
    )
```

profile of v0, /device:TPU:1, one launch (start us, length us, event | category | flops | bytes accessed | tf_op | source)
XLA Modules:
  0.0 493.8 jit_solution(2039549933384206579)
XLA Ops:
  7.2 0.0 all-gather.3.cloned.1.call-start
  7.2 0.7 all-gather.3.cloned.1.call-update
  7.9 0.0 all-gather.5.cloned.1.call-start
  7.9 45.3 %all-gather.3.cloned.1.call-done = bf16[256,3072]{1,0:T(8,128)(2,1)} async-done(((bf16[16,3072]{1,0:T(8,128)(2,1)}), bf16[256,3072]{1,0:T(8,128)(2,1)}) %all-gather.3.cloned.1.call-update) | async-done | bytes 1572880 | tf_op jit(solution)/shard_map/all_gather | solution.py:16
  53.2 0.0 all-gather.5.cloned.1.call-update
  53.2 1.7 copy.7
  55.0 31.8 %all_to_all.19 = bf16[256,4,768]{0,2,1:T(8,128)(2,1)S(1)} all-to-all(bf16[256,4,768]{0,2,1:T(8,128)(2,1)S(1)} %bitcast.6), channel_id=1, replica_groups=mesh['dp'=4,'row'=4,'col'=16] {'dp'}, dimensions={1} | all-to-all | bytes 3145728 | tf_op jit(solution)/shard_map/all_to_all | solution.py:15
  86.8 0.7 copy.8
  87.5 43.1 %all-gather.5.cloned.1.call-done = bf16[1024,3072]{1,0:T(8,128)(2,1)} async-done(((bf16[256,3072]{1,0:T(8,128)(2,1)}), bf16[1024,3072]{1,0:T(8,128)(2,1)}) %all-gather.5.cloned.1.call-update) | async-done | bytes 6291472 | tf_op jit(solution)/shard_map/all_gather | solution.py:18
  130.6 0.0 copy-start.1
  130.6 0.0 copy-start.2
  130.6 11.0 %multiply_reduce_fusion.2 = (f32[3072]{0:T(1024)S(1)}, f32[768]{0:T(1024)S(1)}, f32[3072,768]{1,0:T(8,128)}) fusion(bf16[1024,3072]{1,0:T(8,128)(2,1)} %all-gather.5.cloned.1.call-done, bf16[1024,768]{1,0:T(8,128)(2,1)S(1)} %bitcast.7), kind=kOutput, calls=%fused_computation.3 | convolution fusion | flops 4838912000 | bytes 17316864 | tf_op jit(solution)/shard_map/dot_general | solution.py:17
  141.6 242.3 %psum.28 = f32[3072]{0:T(1024)S(1)} all-reduce(f32[3072]{0:T(1024)S(1)} %get-tuple-element.3), channel_id=1, replica_groups=mesh['dp'=4,'row'=4,'col'=16] {'dp','col'}, use_global_device_ids=true, to_apply=%region_1.0 | all-reduce | flops 3072 | bytes 24576 | tf_op jit(solution)/shard_map/psum | solution.py:24
  383.9 0.0 copy-done.1
  383.9 0.6 fusion.2
  384.5 0.0 copy-start
  384.5 9.1 %all-reduce = (f32[768]{0:T(1024)S(1)}, f32[]{:T(128)}) all-reduce(f32[768]{0:T(1024)S(1)} %get-tuple-element.4, f32[]{:T(128)} %get-tuple-element.9), channel_id=1, replica_groups=mesh['dp'=4,'row'=4,'col'=16] {'row'}, use_global_device_ids=true, to_apply=%region_5.0 | all-reduce | flops 769 | bytes 6152 | tf_op jit(solution)/shard_map/psum | solution.py:27
  394.3 0.0 copy-done.2
  394.3 0.6 fusion.1
  394.9 6.4 %multiply_reduce_fusion = f32[]{:T(128)} fusion(f32[3072,768]{1,0:T(8,128)} %get-tuple-element.11, f32[768]{0:T(1024)S(1)} %get-tuple-element.7, f32[3072]{0:T(1024)S(1)} %divide_rsqrt_fusion), kind=kLoop, calls=%fused_computation | loop fusion | flops 9437183 | bytes 9452548 | tf_op jit(solution)/shard_map/reduce_sum | solution.py:33
  401.3 78.1 %psum.31 = f32[]{:T(128)} all-reduce(f32[]{:T(128)} %multiply_reduce_fusion), channel_id=1, replica_groups=mesh['dp'=4,'row'=4,'col'=16] {'dp','row','col'}, use_global_device_ids=true, to_apply=%region_7.0 | all-reduce | flops 1 | bytes 8 | tf_op jit(solution)/shard_map/psum | solution.py:33
  480.2 6.8 %fusion = f32[3072,768]{1,0:T(8,128)} fusion(f32[3072,768]{1,0:T(8,128)} %get-tuple-element.11, f32[]{:T(128)S(6)} %max.3, f32[768]{0:T(1024)S(1)} %get-tuple-element.7, f32[3072]{0:T(1024)S(1)} %divide_rsqrt_fusion), kind=kLoop, calls=%fused_computation.4 | loop fusion | flops 7077888 | bytes 18889732 | tf_op jit(solution)/shard_map/div | solution.py:35
  487.0 0.0 copy-done
  (1 shorter events, 0.0 us)
Async XLA Ops:
  7.2 46.0 %all-gather.3.cloned.1.call-start = ((), (), s32[]{:S(2)}) async-start(), calls=%async_computation.1 | async-start | bytes 1671168 | tf_op jit(solution)/shard_map/all_gather | solution.py:16
  7.9 122.7 %all-gather.5.cloned.1.call-start = ((), (), s32[]{:S(2)}) async-start(), calls=%async_computation.2 | async-start | bytes 7864320 | tf_op jit(solution)/shard_map/all_gather | solution.py:18
  130.6 253.3 %copy-start.1 = (f32[3072]{0:T(1024)S(1)}, f32[3072]{0:T(1024)}, u32[]{:S(2)}) copy-start(f32[3072]{0:T(1024)} %param.6) | copy-start | bytes 36868
  130.6 263.7 %copy-start.2 = (f32[768]{0:T(1024)S(1)}, f32[768]{0:T(1024)}, u32[]{:S(2)}) copy-start(f32[768]{0:T(1024)} %param.7) | copy-start | bytes 9220
  384.5 102.5 %copy-start = (f32[3072]{0:T(1024)}, f32[3072]{0:T(1024)S(1)}, u32[]{:S(2)}) copy-start(f32[3072]{0:T(1024)S(1)} %get-tuple-element.10) | copy-start | bytes 36868
Sparse Core Ops, SparseCore 0:
  9.8 43.3 all-gather.2
  55.0 75.5 all-gather.4
where the time goes:
time: 494 us
  blocking collectives  361 us (73%)
  waiting for transfers between devices  89.1 us (18%)
  between operations  15.5 us (3%)
  other arithmetic  14.4 us (3%)
  matrix products  11 us (2%)
    psum x1, blocking collectives, on_device(): row_sum = lax.psum(jnp.sum(squared, axis=1), ('dp', 'col'))  242 us
    psum x1, blocking collectives, on_device(): power_sum = lax.psum(jnp.sum(raw_update * raw_update), ('dp', 'row', 'col'))  78.1 us
    all_gather x1, waiting for transfers between devices, on_device(): group_tokens = lax.all_gather(tokens_in, 'col', axis=0, tiled=True)  45.3 us
    all_gather x1, waiting for transfers between devices, on_device(): lax.all_gather(group_tokens, 'dp', axis=0, tiled=True)  43.1 us
    all_to_all x1, blocking collectives, on_device(): lax.all_to_all(out_grad, 'dp', split_axis=1, concat_axis=0, tiled=True)  31.8 us
    dot_general x1, matrix products, on_device(): lax.dot_general(lax.all_gather(group_tokens, 'dp', axis=0, tiled=True), g...  11 us
  transfers between devices with their start and end apart: 2, of which 2 were waited for; matrix products, arithmetic and copies ran while one was open for 0% of the time, Pallas kernels for 0%

commit v1 on v0

v1 whole, which is shorter than its diff:
```python
import jax
import jax.numpy as jnp
from jax import lax
from jax.experimental import pallas as pl
from jax.experimental.pallas import tpu as pltpu
from jax.sharding import Mesh, PartitionSpec as P

D = 12288
F = 49152
DECAY = 0.7
CLIP = 1.0
SIZE = {"dp": 4, "row": 4, "z": 8, "core": 2}
GROUPS = ((0, 3), (3, 5), (5, 7), (7, 8))


SMALL = pltpu.CompilerParams(vmem_limit_bytes=6 * 2**20)


def shift(x, axis, step):
    n = SIZE[axis]
    return lax.ppermute(x, axis, [(i, (i + step) % n) for i in range(n)])


def swap(x):
    return shift(x, "core", 1)


def apart(x, axis, step=1):
    n = SIZE[axis]
    pairs = [(2 * i + c, 2 * ((i + step * (1 - 2 * c)) % n) + c) for i in range(n) for c in (0, 1)]
    return lax.ppermute(x, (axis, "core"), pairs)


def direct(x, axis):
    return [x] + [shift(x, axis, s) for s in range(1, SIZE[axis])]


def flip(x, axis):
    return lax.ppermute(x, axis, [(i, i ^ 1) for i in range(SIZE[axis])])


def four(x, axis, step):
    one = apart(x, axis, step)
    return x, shift(x, axis, 2 * step), one, swap(one)


def grouped(x, axis, step):
    a, b, c, d = four(x, axis, step)
    return (a + b) + (c + d)


def total(x, axis, step):
    return (x + shift(x, axis, 2 * step)) + (shift(x, axis, step) + shift(x, axis, -step))


def order_kernel(place, own, near, far, out):
    z, core, row = place[0], place[1], place[2]
    sign = 2 * core - 1
    offsets = [0] + [o for s in (1, 2, 3) for o in (sign * s, -sign * s)] + [4]
    for slot, offset in enumerate(offsets):
        source = lax.rem(z + offset + 8, 8)
        here = lax.rem(lax.div(source, 4) + row, 2) == 0
        for c in (0, 1):
            inner = pl.multiple_of(lax.rem(source, 4) * 32 + c * 16, 16)
            outer = pl.multiple_of(source * 32 + c * 16, 16)
            base = (slot * 2 + c) * 64
            out[pl.ds(base, 16), :] = own[pl.ds(outer, 16), :]
            for dp in range(3):
                rows = pl.ds(inner, 16)
                value = jnp.where(here, near[dp, rows, :], far[dp, rows, :])
                out[pl.ds(base + (dp + 1) * 16, 16), :] = value


def order(place, own, near, far):
    return pl.pallas_call(
        order_kernel,
        out_shape=jax.ShapeDtypeStruct((1024, 768), jnp.bfloat16),
        in_specs=[pl.BlockSpec(memory_space=pltpu.SMEM)]
        + [pl.BlockSpec(memory_space=pltpu.VMEM)] * 3,
        out_specs=pl.BlockSpec(memory_space=pltpu.VMEM),
        compiler_params=SMALL,
    )(place, own, near, far)


def whole_sum(x):
    return jnp.sum(x, axis=(0, 1), keepdims=True)


def rows_kernel(p0, p1, p2, p3, state, stats, pair):
    parts = (p0[...] + p1[...]) + (p2[...] + p3[...])
    rows = DECAY * state[...] + (1.0 - DECAY) * (parts[:24] / F)
    here = whole_sum(rows) / D
    inverse = lax.rsqrt(rows / here)
    power = whole_sum(parts[24:] * inverse * inverse)
    stats[...] = rows
    pair[0:1, :] = jnp.broadcast_to(here, (1, 128))
    pair[1:2, :] = jnp.broadcast_to(power, (1, 128))


def rows_call(parts, state):
    return pl.pallas_call(
        rows_kernel,
        out_shape=[
            jax.ShapeDtypeStruct((24, 128), jnp.float32),
            jax.ShapeDtypeStruct((2, 128), jnp.float32),
        ],
        in_specs=[pl.BlockSpec(memory_space=pltpu.VMEM)] * 5,
        out_specs=[pl.BlockSpec(memory_space=pltpu.VMEM)] * 2,
        compiler_params=SMALL,
    )(*parts, state)


def update_kernel(p0, p1, p2, p3, stats, scale, grad0, grad1, out, buffer, sems):
    shares = [p[...] for p in (p0, p1, p2, p3)]
    row_mean = (shares[0][0:1] + shares[1][0:1]) + (shares[2][0:1] + shares[3][0:1])
    powers = [p[1:2] * (row_mean / p[0:1]) for p in shares]
    power_sum = (powers[0] + powers[1]) + (powers[2] + powers[3])
    clip_factor = jnp.maximum(1.0, jnp.sqrt(power_sum / (D * F)) / CLIP)
    row_scale = lax.rsqrt(stats[...] / row_mean) / clip_factor
    copies = [None] * 12
    for k in range(12):
        grad = (grad0, grad1)[k // 6]
        if k >= 4:
            copies[k - 4].wait()
        for j in range(2):
            row = row_scale[2 * k + j : 2 * k + j + 1, :]
            down = jnp.transpose(jnp.broadcast_to(row, (128, 128)))
            start = (k % 6) * 256 + j * 128
            for c in range(0, 768, 128):
                value = grad[start : start + 128, c : c + 128] * down
                buffer[k % 4, j * 128 : (j + 1) * 128, c : c + 128] = value * scale[:, c : c + 128]
        copies[k] = pltpu.make_async_copy(
            buffer.at[k % 4], out.at[pl.ds(k * 256, 256), :], sems.at[k % 4]
        )
        copies[k].start()
    for k in range(8, 12):
        copies[k].wait()


def update_call(shares, stats, scale, grads):
    return pl.pallas_call(
        update_kernel,
        out_shape=jax.ShapeDtypeStruct((3072, 768), jnp.float32),
        in_specs=[pl.BlockSpec(memory_space=pltpu.VMEM)] * 8,
        out_specs=pl.BlockSpec(memory_space=pl.ANY),
        scratch_shapes=[
            pltpu.VMEM((4, 256, 768), jnp.float32),
            pltpu.SemaphoreType.DMA((4,)),
        ],
        compiler_params=SMALL,
    )(*shares, stats, scale, *grads)


def on_device(tokens_in, out_grad, row_state, col_state):
    dp, row, z, core = (lax.axis_index(axis) for axis in SIZE)
    first = core == 0

    def by_core(own, other):
        return jnp.where(first, own, other), jnp.where(first, other, own)

    def tie(*values):
        return lax.optimization_barrier(values)

    own = jnp.concatenate(direct(tokens_in, "dp"), axis=0)
    whole = jnp.concatenate(by_core(own, swap(own)), axis=0)
    here = [whole[:, :1536], whole[:, 1536:]]
    halves = [[x] for x in here]

    def units(s, start, size):
        return lax.dynamic_slice(out_grad, (start, ((dp + s) % 4) * 768), (size, 768))

    near = jnp.stack([shift(units(s, row % 2 * 128, 128), "dp", s) for s in (1, 2, 3)])
    parcels = [units(0, 0, 256), near, flip(near, "row")]

    def ring_step(here):
        here = [apart(x, "z") for x in here]
        for half, x in zip(halves, here):
            half += [x, swap(x)]
        return here

    def product(h, lo, hi):
        tokens = jnp.concatenate(halves[h][lo:hi], axis=0)
        rows = b[lo * 128 : hi * 128]
        return lax.dot_general(
            tokens, rows, (((0,), (0,)), ((), ())), preferred_element_type=jnp.float32
        )

    here = ring_step(ring_step(here))
    here, parcels = tie(here, parcels)
    b = order(jnp.stack([z, core, row % 2]), *parcels)
    here = ring_step(here)
    grads = [product(h, 0, 3) for h in (0, 1)]
    here[1], grads = tie(here[1], grads)
    far = apart(by_core(*here)[0], "z")
    grads = [grads[h] + product(h, 3, 7) for h in (0, 1)]
    far, grads = tie(far, grads)
    for half, x in zip(halves, by_core(far, swap(far))):
        half.append(x)
    grads = [grads[h] + product(h, 7, 8) for h in (0, 1)]

    col_part = sum(jnp.sum(grad * grad, axis=0) for grad in grads)
    col_sum = total(col_part, "row", 1)
    col_stats = DECAY * col_state + (1.0 - DECAY) * (col_sum / D)
    col_scale = lax.rsqrt(col_stats)
    scaled = [grad * col_scale[None, :] for grad in grads]
    parts = [jnp.sum(x * x, axis=1).reshape(12, 128) for x in grads + scaled]
    parts = jnp.concatenate(parts, axis=0)
    parts = parts + swap(parts)
    parts = grouped(parts, "dp", 1)
    parts = parts + flip(parts, "z")
    row_stats, pair = rows_call(four(parts, "z", 2), row_state.reshape(24, 128))
    update = update_call(four(pair, "row", 1), row_stats, col_scale.reshape(1, 768), grads)
    return (update, row_stats.reshape(3072), col_stats)


def solution(mesh):
    fine = Mesh(mesh.devices.reshape(4, 4, 8, 2), ("dp", "row", "z", "core"))
    return jax.shard_map(
        on_device,
        mesh=fine,
        in_specs=(
            P(("dp", "z", "core"), "row"),
            P("dp", ("z", "core")),
            P("row"),
            P(("z", "core", "dp")),
        ),
        out_specs=(P("row", ("z", "core", "dp")), P("row"), P(("z", "core", "dp"))),
        check_vma=False,
    )
```

time: 494 us -> 115 us (0.23)
  blocking collectives: 361 us -> 0 us
  waiting for transfers between devices: 89.1 us -> 26 us
  starting transfers between devices: 0.08 us -> 62.4 us
  between operations: 15.5 us -> 1.02 us
  other arithmetic: 14.4 us -> 5.22 us
  Pallas kernels: 0 us -> 5.19 us
    psum x3 -> x0, blocking collectives: 330 us -> none  [the longest x1 242 us: on_device(): row_sum = lax.psum(jnp.sum(squared, axis=1), ('dp', 'col'))]
    all_gather x2 -> x0, waiting for transfers between devices: 88.4 us -> none  [the longest x1 45.3 us: on_device(): group_tokens = lax.all_gather(tokens_in, 'col', axis=0, tiled=True)]
    ppermute x0 -> x36, starting transfers between devices: none -> 62.4 us  [the longest x24 35.4 us: shift(): return lax.ppermute(x, axis, [(i, (i + step) % n) for i in range(n)])]
    all_to_all x1 -> x0, blocking collectives: 31.8 us -> none  [on_device(): lax.all_to_all(out_grad, 'dp', split_axis=1, concat_axis=0, tiled=True)]
    ppermute x0 -> x36, waiting for transfers between devices: none -> 26 us  [the longest x24 13.7 us: shift(): return lax.ppermute(x, axis, [(i, (i + step) % n) for i in range(n)])]
    div x1 -> x0, other arithmetic: 6.82 us -> none  [on_device(): return (raw_update / clip_factor, row_stats, col_stats)]
    pallas_call x0 -> x3, Pallas kernels: none -> 5.19 us  [the longest x1 3.88 us: update_call(): pl.pallas_call(update_kernel, out_shape=jax.ShapeDtypeStruct((3072, 768),...]
    dot_general x1 -> x6, matrix products: 11 us -> 10.5 us  [product(): lax.dot_general(tokens, rows, (((0,), (0,)), ((), ())), preferred_element...]
  transfers between devices with their start and end apart: 2 -> 36, of which waited for: 2 -> 17; matrix products, arithmetic and copies ran while one was open for 0% -> 11% of each run, Pallas kernels for 0% -> 1%
where the time goes in v1:
time: 115 us; the launch traced here: 114 us
  starting transfers between devices  62.4 us (54%)
  waiting for transfers between devices  26 us (23%)
  matrix products  10.5 us (9%)
  other arithmetic  5.22 us (5%)
  Pallas kernels  5.19 us (5%)
  local copies, waits for them, and re-layouts  3.86 us (3%)
    ppermute x24, starting transfers between devices, shift(): return lax.ppermute(x, axis, [(i, (i + step) % n) for i in range(n)])  35.4 us
    ppermute x10, starting transfers between devices, apart(): return lax.ppermute(x, (axis, 'core'), pairs)  25.6 us
    ppermute x24, waiting for transfers between devices, shift(): return lax.ppermute(x, axis, [(i, (i + step) % n) for i in range(n)])  13.7 us
    dot_general x6, matrix products, product(): lax.dot_general(tokens, rows, (((0,), (0,)), ((), ())), preferred_element...  10.5 us
    ppermute x2, waiting for transfers between devices, flip(): return lax.ppermute(x, axis, [(i, i ^ 1) for i in range(SIZE[axis])])  6.47 us
    ppermute x10, waiting for transfers between devices, apart(): return lax.ppermute(x, (axis, 'core'), pairs)  5.86 us
    reduce_sum x2, other arithmetic, on_device(): parts = [jnp.sum(x * x, axis=1).reshape(12, 128) for x in grads + scaled]  4.29 us
    pallas_call x1, Pallas kernels, update_call(): pl.pallas_call(update_kernel, out_shape=jax.ShapeDtypeStruct((3072, 768),...  3.88 us
  transfers between devices with their start and end apart: 36, of which 17 were waited for; matrix products, arithmetic and copies ran while one was open for 11% of the time, Pallas kernels for 1%

profile of v1, /device:TPU:1, one launch (start us, length us, event | category | flops | bytes accessed | tf_op | source)
XLA Modules:
  0.0 114.2 jit_solution(7608830001486334605)
XLA Ops:
  0.6 3.8 %collective-permute-start.1 = (bf16[16,3072]{1,0:T(8,128)(2,1)}, bf16[16,3072]{1,0:T(8,128)(2,1)S(1)}, u32[]{:S(2)}, u32[]{:S(2)}) collective-permute-start(bf16[16,3072]{1,0:T(8,128)(2,1)} %param.4), channel_id=1, source_target_pairs={{0,128},{64,192},{128,0},{192,64},{1,129},{65,193},{129,1},{193,65... | collective-permute-start | bytes 294920 | tf_op jit(solution)/shard_map/ppermute | solution.py:21
  4.9 2.3 %collective-permute-start.2 = (bf16[16,3072]{1,0:T(8,128)(2,1)}, bf16[16,3072]{1,0:T(8,128)(2,1)S(1)}, u32[]{:S(2)}, u32[]{:S(2)}) collective-permute-start(bf16[16,3072]{1,0:T(8,128)(2,1)} %param.4), channel_id=1, source_target_pairs={{0,192},{64,0},{128,64},{192,128},{1,193},{65,1},{129,65},{193,129... | collective-permute-start | bytes 294920 | tf_op jit(solution)/shard_map/ppermute | solution.py:21
  8.1 3.2 %collective-permute-done = bf16[16,3072]{1,0:T(8,128)(2,1)S(1)} collective-permute-done((bf16[16,3072]{1,0:T(8,128)(2,1)}, bf16[16,3072]{1,0:T(8,128)(2,1)S(1)}, u32[]{:S(2)}, u32[]{:S(2)}) %collective-permute-start) | collective-permute-done | bytes 98336 | tf_op jit(solution)/shard_map/ppermute | solution.py:21
  13.5 2.7 %collective-permute-start.10 = (bf16[128,768]{1,0:T(8,128)(2,1)S(1)}, bf16[128,768]{1,0:T(8,128)(2,1)S(1)}, u32[]{:S(2)}, u32[]{:S(2)}) collective-permute-start(bf16[128,768]{1,0:T(8,128)(2,1)S(1)} %get-tuple-element.40), channel_id=1, source_target_pairs={{0,192},{64,0},{128,64},{192,128},{1,193},{65,1},{129,65},{193,129... | collective-permute-start | bytes 589832 | tf_op jit(solution)/shard_map/ppermute | solution.py:21
  17.1 5.7 %collective-permute-start.6 = (bf16[128,1536]{1,0:T(8,128)(2,1)S(1)}, bf16[128,1536]{1,0:T(8,128)(2,1)S(1)}, u32[]{:S(2)}, u32[]{:S(2)}) collective-permute-start(bf16[128,1536]{1,0:T(8,128)(2,1)S(1)} %get-tuple-element.42), channel_id=1, source_target_pairs={{0,2},{1,15},{2,4},{3,1},{4,6},{5,3},{6,8},{7,5},{8,10},{9,7},{10,... | collective-permute-start | bytes 1179656 | tf_op jit(solution)/shard_map/ppermute | solution.py:31
  24.2 1.9 %collective-permute-done.9 = bf16[128,768]{1,0:T(8,128)(2,1)S(1)} collective-permute-done((bf16[128,768]{1,0:T(8,128)(2,1)S(1)}, bf16[128,768]{1,0:T(8,128)(2,1)S(1)}, u32[]{:S(2)}, u32[]{:S(2)}) %collective-permute-start.9) | collective-permute-done | bytes 196640 | tf_op jit(solution)/shard_map/ppermute | solution.py:21
  27.5 5.6 %collective-permute-start.7 = (bf16[128,1536]{1,0:T(8,128)(2,1)S(1)}, bf16[128,1536]{1,0:T(8,128)(2,1)S(1)}, u32[]{:S(2)}, u32[]{:S(2)}) collective-permute-start(bf16[128,1536]{1,0:T(8,128)(2,1)S(1)} %collective-permute-done.6), channel_id=1, source_target_pairs={{0,2},{1,15},{2,4},{3,1},{4,6},{5,3},{6,8},{7,5},{8,10},{9,7},{10,... | collective-permute-start | bytes 1179656 | tf_op jit(solution)/shard_map/ppermute | solution.py:31
  33.1 1.7 %collective-permute-start.5 = (bf16[128,1536]{1,0:T(8,128)(2,1)S(1)}, bf16[128,1536]{1,0:T(8,128)(2,1)S(1)}, u32[]{:S(2)}, u32[]{:S(2)}) collective-permute-start(bf16[128,1536]{1,0:T(8,128)(2,1)S(1)} %collective-permute-done.4), channel_id=1, source_target_pairs={{0,2},{1,15},{2,4},{3,1},{4,6},{5,3},{6,8},{7,5},{8,10},{9,7},{10,... | collective-permute-start | bytes 1179656 | tf_op jit(solution)/shard_map/ppermute | solution.py:31
  36.5 3.8 %collective-permute-done.11.far = bf16[3,128,768]{2,1,0:T(8,128)(2,1)S(1)} collective-permute-done((bf16[3,128,768]{2,1,0:T(8,128)(2,1)S(1)}, bf16[3,128,768]{2,1,0:T(8,128)(2,1)S(1)}, u32[]{:S(2)}, u32[]{:S(2)}) %collective-permute-start.11) | collective-permute-done | bytes 589856 | tf_op jit(solution)/shard_map/ppermute | solution.py:39
  40.3 1.7 %collective-permute-done.5 = bf16[128,1536]{1,0:T(8,128)(2,1)S(1)} collective-permute-done((bf16[128,1536]{1,0:T(8,128)(2,1)S(1)}, bf16[128,1536]{1,0:T(8,128)(2,1)S(1)}, u32[]{:S(2)}, u32[]{:S(2)}) %collective-permute-start.5) | collective-permute-done | bytes 393248 | tf_op jit(solution)/shard_map/ppermute | solution.py:31
  42.0 3.8 %collective-permute-start.12 = (bf16[128,1536]{1,0:T(8,128)(2,1)S(1)}, bf16[128,1536]{1,0:T(8,128)(2,1)S(1)}, u32[]{:S(2)}, u32[]{:S(2)}) collective-permute-start(bf16[128,1536]{1,0:T(8,128)(2,1)S(1)} %collective-permute-done.5), channel_id=1, source_target_pairs={{0,2},{1,15},{2,4},{3,1},{4,6},{5,3},{6,8},{7,5},{8,10},{9,7},{10,... | collective-permute-start | bytes 1179656 | tf_op jit(solution)/shard_map/ppermute | solution.py:31
  47.9 2.4 %fusion.20 = f32[1536,768]{1,0:T(8,128)S(1)} fusion(bf16[128,1536]{1,0:T(8,128)(2,1)} %collective-permute-done.15, bf16[128,1536]{1,0:T(8,128)(2,1)S(1)} %collective-permute-done.6, bf16[128,1536]{1,0:T(8,128)(2,1)S(1)} %get-tuple-element.42, bf16[1024,768]{1,0:T(8,128)(2,1)S(1)} %shard_map.67), kind=kOutput, calls=%fused_computation.28 | convolution fusion | flops 909508608 | bytes 6488064 | tf_op jit(solution)/shard_map/dot_general | solution.py:184
  50.3 1.4 %fusion.14 = f32[1536,768]{1,0:T(8,128)S(1)} fusion(bf16[128,1536]{1,0:T(8,128)(2,1)S(1)} %collective-permute-done.14, bf16[128,1536]{1,0:T(8,128)(2,1)S(1)} %collective-permute-done.4, bf16[128,1536]{1,0:T(8,128)(2,1)S(1)} %get-tuple-element.43, bf16[1024,768]{1,0:T(8,128)(2,1)S(1)} %shard_map.67), kind=kOutput, calls=%fused_computation.22 | convolution fusion | flops 909508608 | bytes 6488064 | tf_op jit(solution)/shard_map/dot_general | solution.py:184
  51.8 3.0 %collective-permute-done.13 = bf16[128,1536]{1,0:T(8,128)(2,1)S(1)} collective-permute-done((bf16[128,1536]{1,0:T(8,128)(2,1)S(1)}, bf16[128,1536]{1,0:T(8,128)(2,1)S(1)}, u32[]{:S(2)}, u32[]{:S(2)}) %collective-permute-start.13) | collective-permute-done | bytes 393248 | tf_op jit(solution)/shard_map/ppermute | solution.py:31
  54.8 3.1 %collective-permute-start.18 = (bf16[128,1536]{1,0:T(8,128)(2,1)S(1)}, bf16[128,1536]{1,0:T(8,128)(2,1)S(1)}, u32[]{:S(2)}, u32[]{:S(2)}) collective-permute-start(bf16[128,1536]{1,0:T(8,128)(2,1)S(1)} %collective-permute-done.12), channel_id=1, source_target_pairs={{0,1},{1,0},{2,3},{3,2},{4,5},{5,4},{6,7},{7,6},{8,9},{9,8},{10,11... | collective-permute-start | bytes 1179656 | tf_op jit(solution)/shard_map/ppermute | solution.py:21
  57.9 1.8 %collective-permute-start.16 = (bf16[128,1536]{1,0:T(8,128)(2,1)S(1)}, bf16[128,1536]{1,0:T(8,128)(2,1)S(1)}, u32[]{:S(2)}, u32[]{:S(2)}) collective-permute-start(bf16[128,1536]{1,0:T(8,128)(2,1)S(1)} %broadcast_select_fusion.2), channel_id=1, source_target_pairs={{0,2},{1,15},{2,4},{3,1},{4,6},{5,3},{6,8},{7,5},{8,10},{9,7},{10,... | collective-permute-start | bytes 1179656 | tf_op jit(solution)/shard_map/ppermute | solution.py:31
  59.8 1.4 %convolution_add_fusion.1 = f32[1536,768]{1,0:T(8,128)S(1)} fusion(f32[1536,768]{1,0:T(8,128)S(1)} %fusion.14, bf16[128,1536]{1,0:T(8,128)(2,1)S(1)} %collective-permute-done.18, bf16[128,1536]{1,0:T(8,128)(2,1)S(1)} %collective-permute-done.12, bf16[128,1536]{1,0:T(8,128)(2,1)S(1)} %collective-permute-done.17, ...), kind=kOutput, calls=%fused_computation.7 | convolution fusion | flops 1215430656 | bytes 11796480 | tf_op jit(solution)/shard_map/dot_general | solution.py:184
  61.5 3.6 %convolution_add_fusion = f32[1536,768]{1,0:T(8,128)} fusion(f32[1536,768]{1,0:T(8,128)S(1)} %fusion.20, bf16[128,1536]{1,0:T(8,128)(2,1)S(1)} %collective-permute-done.20, bf16[128,1536]{1,0:T(8,128)(2,1)S(1)} %collective-permute-done.13, bf16[128,1536]{1,0:T(8,128)(2,1)S(1)} %collective-permute-done.19, bf16[128,1536]{1,0:T(8,128)(2,1)S(1)} %collective-permute-done.7, ...), kind=kOutput, calls=%fused_computation.6 | convolution fusion | flops 1215430656 | bytes 11796480 | tf_op jit(solution)/shard_map/dot_general | solution.py:184
  65.1 1.9 %collective-permute-start.21 = (bf16[128,1536]{1,0:T(8,128)(2,1)S(1)}, bf16[128,1536]{1,0:T(8,128)(2,1)S(1)}, u32[]{:S(2)}, u32[]{:S(2)}) collective-permute-start(bf16[128,1536]{1,0:T(8,128)(2,1)S(1)} %collective-permute-done.16), channel_id=1, source_target_pairs={{0,1},{1,0},{2,3},{3,2},{4,5},{5,4},{6,7},{7,6},{8,9},{9,8},{10,11... | collective-permute-start | bytes 1179656 | tf_op jit(solution)/shard_map/ppermute | solution.py:21
  70.0 3.3 %multiply_reduce_fusion.3 = (f32[1536]{0:T(1024)S(1)}, f32[768]{0:T(1024)S(1)}, f32[1536,768]{1,0:T(8,128)S(1)}, f32[768]{0:T(1024)S(1)}, f32[1536]{0:T(1024)S(1)}, /*index=5*/f32[1536,768]{1,0:T(8,128)S(1)}) fusion(f32[1536,768]{1,0:T(8,128)} %convolution_add_fusion, f32[1536,768]{1,0:T(8,128)S(1)} %fusion.31, f32[1536,768]{1,0:T(8,128)S(1)} %convolution_add_fusion.1, ...), kind=kLoop, calls=%fused_computation.3 | loop fusion | flops 9432576 | bytes 28329984 | tf_op jit(solution)/shard_map/reduce_sum | solution.py:206
  73.3 2.6 %collective-permute-start.24 = (f32[768]{0:T(1024)S(1)}, f32[768]{0:T(1024)S(1)}, u32[]{:S(2)}, u32[]{:S(2)}) collective-permute-start(f32[768]{0:T(1024)S(1)} %add.104), channel_id=1, source_target_pairs={{0,48},{16,0},{32,16},{48,32},{1,49},{17,1},{33,17},{49,33},{2,50}... | collective-permute-start | bytes 9224 | tf_op jit(solution)/shard_map/ppermute | solution.py:21
  75.8 1.7 %collective-permute-start.22 = (f32[768]{0:T(1024)S(1)}, f32[768]{0:T(1024)S(1)}, u32[]{:S(2)}, u32[]{:S(2)}) collective-permute-start(f32[768]{0:T(1024)S(1)} %add.104), channel_id=1, source_target_pairs={{0,32},{16,48},{32,0},{48,16},{1,33},{17,49},{33,1},{49,17},{2,34}... | collective-permute-start | bytes 9224 | tf_op jit(solution)/shard_map/ppermute | solution.py:21
  77.6 1.9 %collective-permute-done.23 = f32[768]{0:T(1024)S(1)} collective-permute-done((f32[768]{0:T(1024)S(1)}, f32[768]{0:T(1024)S(1)}, u32[]{:S(2)}, u32[]{:S(2)}) %collective-permute-start.23) | collective-permute-done | bytes 3104 | tf_op jit(solution)/shard_map/ppermute | solution.py:21
  81.4 1.9 %collective-permute-start.25 = (f32[48,128]{1,0:T(8,128)S(1)}, f32[48,128]{1,0:T(8,128)S(1)}, u32[]{:S(2)}, u32[]{:S(2)}) collective-permute-start(f32[48,128]{1,0:T(8,128)S(1)} %pad_maximum_fusion.2), channel_id=1, source_target_pairs={{0,1},{1,0},{2,3},{3,2},{4,5},{5,4},{6,7},{7,6},{8,9},{9,8},{10,11... | collective-permute-start | bytes 73736 | tf_op jit(solution)/shard_map/ppermute | solution.py:21
  84.2 1.7 %collective-permute-start.27 = (f32[48,128]{1,0:T(8,128)S(1)}, f32[48,128]{1,0:T(8,128)S(1)}, u32[]{:S(2)}, u32[]{:S(2)}) collective-permute-start(f32[48,128]{1,0:T(8,128)S(1)} %fusion.45), channel_id=1, source_target_pairs={{0,64},{1,193},{64,128},{65,1},{128,192},{129,65},{192,0},{193,129... | collective-permute-start | bytes 73736 | tf_op jit(solution)/shard_map/ppermute | solution.py:31
  86.9 2.7 %collective-permute-start.28 = (f32[48,128]{1,0:T(8,128)S(1)}, f32[48,128]{1,0:T(8,128)S(1)}, u32[]{:S(2)}, u32[]{:S(2)}) collective-permute-start(f32[48,128]{1,0:T(8,128)S(1)} %collective-permute-done.27), channel_id=1, source_target_pairs={{0,1},{1,0},{2,3},{3,2},{4,5},{5,4},{6,7},{7,6},{8,9},{9,8},{10,11... | collective-permute-start | bytes 73736 | tf_op jit(solution)/shard_map/ppermute | solution.py:21
  90.7 2.7 %collective-permute-done.29 = f32[48,128]{1,0:T(8,128)S(1)} collective-permute-done((f32[48,128]{1,0:T(8,128)S(1)}, f32[48,128]{1,0:T(8,128)S(1)}, u32[]{:S(2)}, u32[]{:S(2)}) %collective-permute-start.29) | collective-permute-done | bytes 24608 | tf_op jit(solution)/shard_map/ppermute | solution.py:39
  94.3 3.4 %collective-permute-start.30 = (f32[48,128]{1,0:T(8,128)S(1)}, f32[48,128]{1,0:T(8,128)S(1)}, u32[]{:S(2)}, u32[]{:S(2)}) collective-permute-start(f32[48,128]{1,0:T(8,128)S(1)} %add.113.p0), channel_id=1, source_target_pairs={{0,8},{2,10},{4,12},{6,14},{8,0},{10,2},{12,4},{14,6},{1,9},{3,11}... | collective-permute-start | bytes 73736 | tf_op jit(solution)/shard_map/ppermute | solution.py:21
  97.7 3.4 %collective-permute-start.32 = (f32[48,128]{1,0:T(8,128)S(1)}, f32[48,128]{1,0:T(8,128)S(1)}, u32[]{:S(2)}, u32[]{:S(2)}) collective-permute-start(f32[48,128]{1,0:T(8,128)S(1)} %collective-permute-done.31.p2), channel_id=1, source_target_pairs={{0,1},{1,0},{2,3},{3,2},{4,5},{5,4},{6,7},{7,6},{8,9},{9,8},{10,11... | collective-permute-start | bytes 73736 | tf_op jit(solution)/shard_map/ppermute | solution.py:21
  102.5 3.0 %collective-permute-start.34 = (f32[2,128]{1,0:T(2,128)S(1)}, f32[2,128]{1,0:T(2,128)S(1)}, u32[]{:S(2)}, u32[]{:S(2)}) collective-permute-start(f32[2,128]{1,0:T(2,128)S(1)} %get-tuple-element.27.p0), channel_id=1, source_target_pairs={{0,16},{1,49},{16,32},{17,1},{32,48},{33,17},{48,0},{49,33},{2,18}... | collective-permute-start | bytes 3080 | tf_op jit(solution)/shard_map/ppermute | solution.py:31
  106.2 1.9 %collective-permute-start.35 = (f32[2,128]{1,0:T(2,128)S(1)}, f32[2,128]{1,0:T(2,128)S(1)}, u32[]{:S(2)}, u32[]{:S(2)}) collective-permute-start(f32[2,128]{1,0:T(2,128)S(1)} %collective-permute-done.34.p2), channel_id=1, source_target_pairs={{0,1},{1,0},{2,3},{3,2},{4,5},{5,4},{6,7},{7,6},{8,9},{9,8},{10,11... | collective-permute-start | bytes 3080 | tf_op jit(solution)/shard_map/ppermute | solution.py:21
  110.1 3.9 %shard_map.69 = f32[3072,768]{1,0:T(8,128)} custom-call(f32[2,128]{1,0:T(2,128)S(1)} %get-tuple-element.27.p0, f32[2,128]{1,0:T(2,128)S(1)} %collective-permute-done.33.p1, f32[2,128]{1,0:T(2,128)S(1)} %collective-permute-done.34.p2, f32[2,128]{1,0:T(2,128)S(1)} %collective-permute-done.35.p3, f32[24,128]{1,0:T(8,128)S(1)} %copy-done, ...), custom_call_target="tpu_custom_call" | custom-call | tf_op jit(solution)/shard_map/pallas_call | solution.py:141
  (75 shorter events, 24.3 us)
Async XLA Ops:
  0.6 10.7 %collective-permute-start.1 = (bf16[16,3072]{1,0:T(8,128)(2,1)}, bf16[16,3072]{1,0:T(8,128)(2,1)S(1)}, u32[]{:S(2)}, u32[]{:S(2)}) collective-permute-start(bf16[16,3072]{1,0:T(8,128)(2,1)} %param.4), channel_id=1, source_target_pairs={{0,128},{64,192},{128,0},{192,64},{1,129},{65,193},{129,1},{193,65... | collective-permute-start | bytes 294920 | tf_op jit(solution)/shard_map/ppermute | solution.py:21
  4.5 6.9 %collective-permute-start = (bf16[16,3072]{1,0:T(8,128)(2,1)}, bf16[16,3072]{1,0:T(8,128)(2,1)S(1)}, u32[]{:S(2)}, u32[]{:S(2)}) collective-permute-start(bf16[16,3072]{1,0:T(8,128)(2,1)} %param.4), channel_id=1, source_target_pairs={{0,64},{64,128},{128,192},{192,0},{1,65},{65,129},{129,193},{193,1... | collective-permute-start | bytes 294920 | tf_op jit(solution)/shard_map/ppermute | solution.py:21
  4.9 6.5 %collective-permute-start.2 = (bf16[16,3072]{1,0:T(8,128)(2,1)}, bf16[16,3072]{1,0:T(8,128)(2,1)S(1)}, u32[]{:S(2)}, u32[]{:S(2)}) collective-permute-start(bf16[16,3072]{1,0:T(8,128)(2,1)} %param.4), channel_id=1, source_target_pairs={{0,192},{64,0},{128,64},{192,128},{1,193},{65,1},{129,65},{193,129... | collective-permute-start | bytes 294920 | tf_op jit(solution)/shard_map/ppermute | solution.py:21
  11.4 5.6 %collective-permute-start.3 = (bf16[64,3072]{1,0:T(8,128)(2,1)S(1)}, bf16[64,3072]{1,0:T(8,128)(2,1)S(1)}, u32[]{:S(2)}, u32[]{:S(2)}) collective-permute-start(bf16[64,3072]{1,0:T(8,128)(2,1)S(1)} %constant_dynamic-update-slice_fusion), channel_id=1, source_target_pairs={{0,1},{1,0},{2,3},{3,2},{4,5},{5,4},{6,7},{7,6},{8,9},{9,8},{10,11... | collective-permute-start | bytes 1179656 | tf_op jit(solution)/shard_map/ppermute | solution.py:21
  13.5 10.0 %collective-permute-start.8 = (bf16[128,768]{1,0:T(8,128)(2,1)S(1)}, bf16[128,768]{1,0:T(8,128)(2,1)S(1)}, u32[]{:S(2)}, u32[]{:S(2)}) collective-permute-start(bf16[128,768]{1,0:T(8,128)(2,1)S(1)} %get-tuple-element.39), channel_id=1, source_target_pairs={{0,64},{64,128},{128,192},{192,0},{1,65},{65,129},{129,193},{193,1... | collective-permute-start | bytes 589832 | tf_op jit(solution)/shard_map/ppermute | solution.py:21
  13.5 10.7 %collective-permute-start.10 = (bf16[128,768]{1,0:T(8,128)(2,1)S(1)}, bf16[128,768]{1,0:T(8,128)(2,1)S(1)}, u32[]{:S(2)}, u32[]{:S(2)}) collective-permute-start(bf16[128,768]{1,0:T(8,128)(2,1)S(1)} %get-tuple-element.40), channel_id=1, source_target_pairs={{0,192},{64,0},{128,64},{192,128},{1,193},{65,1},{129,65},{193,129... | collective-permute-start | bytes 589832 | tf_op jit(solution)/shard_map/ppermute | solution.py:21
  16.2 9.9 %collective-permute-start.9 = (bf16[128,768]{1,0:T(8,128)(2,1)S(1)}, bf16[128,768]{1,0:T(8,128)(2,1)S(1)}, u32[]{:S(2)}, u32[]{:S(2)}) collective-permute-start(bf16[128,768]{1,0:T(8,128)(2,1)S(1)} %get-tuple-element.41), channel_id=1, source_target_pairs={{0,128},{64,192},{128,0},{192,64},{1,129},{65,193},{129,1},{193,65... | collective-permute-start | bytes 589832 | tf_op jit(solution)/shard_map/ppermute | solution.py:21
  17.1 10.4 %collective-permute-start.6 = (bf16[128,1536]{1,0:T(8,128)(2,1)S(1)}, bf16[128,1536]{1,0:T(8,128)(2,1)S(1)}, u32[]{:S(2)}, u32[]{:S(2)}) collective-permute-start(bf16[128,1536]{1,0:T(8,128)(2,1)S(1)} %get-tuple-element.42), channel_id=1, source_target_pairs={{0,2},{1,15},{2,4},{3,1},{4,6},{5,3},{6,8},{7,5},{8,10},{9,7},{10,... | collective-permute-start | bytes 1179656 | tf_op jit(solution)/shard_map/ppermute | solution.py:31
  22.7 10.4 %collective-permute-start.4 = (bf16[128,1536]{1,0:T(8,128)(2,1)S(1)}, bf16[128,1536]{1,0:T(8,128)(2,1)S(1)}, u32[]{:S(2)}, u32[]{:S(2)}) collective-permute-start(bf16[128,1536]{1,0:T(8,128)(2,1)S(1)} %get-tuple-element.43), channel_id=1, source_target_pairs={{0,2},{1,15},{2,4},{3,1},{4,6},{5,3},{6,8},{7,5},{8,10},{9,7},{10,... | collective-permute-start | bytes 1179656 | tf_op jit(solution)/shard_map/ppermute | solution.py:31
  26.2 14.1 %collective-permute-start.11 = (bf16[3,128,768]{2,1,0:T(8,128)(2,1)S(1)}, bf16[3,128,768]{2,1,0:T(8,128)(2,1)S(1)}, u32[]{:S(2)}, u32[]{:S(2)}) collective-permute-start(bf16[3,128,768]{2,1,0:T(8,128)(2,1)S(1)} %pad_maximum_fusion.near), channel_id=1, source_target_pairs={{0,16},{16,0},{32,48},{48,32},{1,17},{17,1},{33,49},{49,33},{2,18}... | collective-permute-start | bytes 1769480 | tf_op jit(solution)/shard_map/ppermute | solution.py:39
  27.5 12.8 %collective-permute-start.7 = (bf16[128,1536]{1,0:T(8,128)(2,1)S(1)}, bf16[128,1536]{1,0:T(8,128)(2,1)S(1)}, u32[]{:S(2)}, u32[]{:S(2)}) collective-permute-start(bf16[128,1536]{1,0:T(8,128)(2,1)S(1)} %collective-permute-done.6), channel_id=1, source_target_pairs={{0,2},{1,15},{2,4},{3,1},{4,6},{5,3},{6,8},{7,5},{8,10},{9,7},{10,... | collective-permute-start | bytes 1179656 | tf_op jit(solution)/shard_map/ppermute | solution.py:31
  33.1 8.9 %collective-permute-start.5 = (bf16[128,1536]{1,0:T(8,128)(2,1)S(1)}, bf16[128,1536]{1,0:T(8,128)(2,1)S(1)}, u32[]{:S(2)}, u32[]{:S(2)}) collective-permute-start(bf16[128,1536]{1,0:T(8,128)(2,1)S(1)} %collective-permute-done.4), channel_id=1, source_target_pairs={{0,2},{1,15},{2,4},{3,1},{4,6},{5,3},{6,8},{7,5},{8,10},{9,7},{10,... | collective-permute-start | bytes 1179656 | tf_op jit(solution)/shard_map/ppermute | solution.py:31
  34.8 12.6 %collective-permute-start.15 = (bf16[128,1536]{1,0:T(8,128)(2,1)S(1)}, bf16[128,1536]{1,0:T(8,128)(2,1)}, u32[]{:S(2)}, u32[]{:S(2)}) collective-permute-start(bf16[128,1536]{1,0:T(8,128)(2,1)S(1)} %collective-permute-done.6), channel_id=1, source_target_pairs={{0,1},{1,0},{2,3},{3,2},{4,5},{5,4},{6,7},{7,6},{8,9},{9,8},{10,11... | collective-permute-start | bytes 1179656 | tf_op jit(solution)/shard_map/ppermute | solution.py:21
  35.8 14.5 %collective-permute-start.14 = (bf16[128,1536]{1,0:T(8,128)(2,1)S(1)}, bf16[128,1536]{1,0:T(8,128)(2,1)S(1)}, u32[]{:S(2)}, u32[]{:S(2)}) collective-permute-start(bf16[128,1536]{1,0:T(8,128)(2,1)S(1)} %collective-permute-done.4), channel_id=1, source_target_pairs={{0,1},{1,0},{2,3},{3,2},{4,5},{5,4},{6,7},{7,6},{8,9},{9,8},{10,11... | collective-permute-start | bytes 1179656 | tf_op jit(solution)/shard_map/ppermute | solution.py:21
  42.0 12.8 %collective-permute-start.12 = (bf16[128,1536]{1,0:T(8,128)(2,1)S(1)}, bf16[128,1536]{1,0:T(8,128)(2,1)S(1)}, u32[]{:S(2)}, u32[]{:S(2)}) collective-permute-start(bf16[128,1536]{1,0:T(8,128)(2,1)S(1)} %collective-permute-done.5), channel_id=1, source_target_pairs={{0,2},{1,15},{2,4},{3,1},{4,6},{5,3},{6,8},{7,5},{8,10},{9,7},{10,... | collective-permute-start | bytes 1179656 | tf_op jit(solution)/shard_map/ppermute | solution.py:31
  45.9 8.9 %collective-permute-start.13 = (bf16[128,1536]{1,0:T(8,128)(2,1)S(1)}, bf16[128,1536]{1,0:T(8,128)(2,1)S(1)}, u32[]{:S(2)}, u32[]{:S(2)}) collective-permute-start(bf16[128,1536]{1,0:T(8,128)(2,1)S(1)} %collective-permute-done.7), channel_id=1, source_target_pairs={{0,2},{1,15},{2,4},{3,1},{4,6},{5,3},{6,8},{7,5},{8,10},{9,7},{10,... | collective-permute-start | bytes 1179656 | tf_op jit(solution)/shard_map/ppermute | solution.py:31
  47.3 13.9 %collective-permute-start.19 = (bf16[128,1536]{1,0:T(8,128)(2,1)S(1)}, bf16[128,1536]{1,0:T(8,128)(2,1)S(1)}, u32[]{:S(2)}, u32[]{:S(2)}) collective-permute-start(bf16[128,1536]{1,0:T(8,128)(2,1)S(1)} %collective-permute-done.7), channel_id=1, source_target_pairs={{0,1},{1,0},{2,3},{3,2},{4,5},{5,4},{6,7},{7,6},{8,9},{9,8},{10,11... | collective-permute-start | bytes 1179656 | tf_op jit(solution)/shard_map/ppermute | solution.py:21
  47.4 12.3 %collective-permute-start.17 = (bf16[128,1536]{1,0:T(8,128)(2,1)S(1)}, bf16[128,1536]{1,0:T(8,128)(2,1)S(1)}, u32[]{:S(2)}, u32[]{:S(2)}) collective-permute-start(bf16[128,1536]{1,0:T(8,128)(2,1)S(1)} %collective-permute-done.5), channel_id=1, source_target_pairs={{0,1},{1,0},{2,3},{3,2},{4,5},{5,4},{6,7},{7,6},{8,9},{9,8},{10,11... | collective-permute-start | bytes 1179656 | tf_op jit(solution)/shard_map/ppermute | solution.py:21
  54.8 5.0 %collective-permute-start.18 = (bf16[128,1536]{1,0:T(8,128)(2,1)S(1)}, bf16[128,1536]{1,0:T(8,128)(2,1)S(1)}, u32[]{:S(2)}, u32[]{:S(2)}) collective-permute-start(bf16[128,1536]{1,0:T(8,128)(2,1)S(1)} %collective-permute-done.12), channel_id=1, source_target_pairs={{0,1},{1,0},{2,3},{3,2},{4,5},{5,4},{6,7},{7,6},{8,9},{9,8},{10,11... | collective-permute-start | bytes 1179656 | tf_op jit(solution)/shard_map/ppermute | solution.py:21
  57.9 7.2 %collective-permute-start.16 = (bf16[128,1536]{1,0:T(8,128)(2,1)S(1)}, bf16[128,1536]{1,0:T(8,128)(2,1)S(1)}, u32[]{:S(2)}, u32[]{:S(2)}) collective-permute-start(bf16[128,1536]{1,0:T(8,128)(2,1)S(1)} %broadcast_select_fusion.2), channel_id=1, source_target_pairs={{0,2},{1,15},{2,4},{3,1},{4,6},{5,3},{6,8},{7,5},{8,10},{9,7},{10,... | collective-permute-start | bytes 1179656 | tf_op jit(solution)/shard_map/ppermute | solution.py:31
  65.1 3.3 %collective-permute-start.21 = (bf16[128,1536]{1,0:T(8,128)(2,1)S(1)}, bf16[128,1536]{1,0:T(8,128)(2,1)S(1)}, u32[]{:S(2)}, u32[]{:S(2)}) collective-permute-start(bf16[128,1536]{1,0:T(8,128)(2,1)S(1)} %collective-permute-done.16), channel_id=1, source_target_pairs={{0,1},{1,0},{2,3},{3,2},{4,5},{5,4},{6,7},{7,6},{8,9},{9,8},{10,11... | collective-permute-start | bytes 1179656 | tf_op jit(solution)/shard_map/ppermute | solution.py:21
  73.3 4.3 %collective-permute-start.24 = (f32[768]{0:T(1024)S(1)}, f32[768]{0:T(1024)S(1)}, u32[]{:S(2)}, u32[]{:S(2)}) collective-permute-start(f32[768]{0:T(1024)S(1)} %add.104), channel_id=1, source_target_pairs={{0,48},{16,0},{32,16},{48,32},{1,49},{17,1},{33,17},{49,33},{2,50}... | collective-permute-start | bytes 9224 | tf_op jit(solution)/shard_map/ppermute | solution.py:21
  75.8 3.7 %collective-permute-start.23 = (f32[768]{0:T(1024)S(1)}, f32[768]{0:T(1024)S(1)}, u32[]{:S(2)}, u32[]{:S(2)}) collective-permute-start(f32[768]{0:T(1024)S(1)} %add.104), channel_id=1, source_target_pairs={{0,16},{16,32},{32,48},{48,0},{1,17},{17,33},{33,49},{49,1},{2,18}... | collective-permute-start | bytes 9224 | tf_op jit(solution)/shard_map/ppermute | solution.py:21
  75.8 4.0 %collective-permute-start.22 = (f32[768]{0:T(1024)S(1)}, f32[768]{0:T(1024)S(1)}, u32[]{:S(2)}, u32[]{:S(2)}) collective-permute-start(f32[768]{0:T(1024)S(1)} %add.104), channel_id=1, source_target_pairs={{0,32},{16,48},{32,0},{48,16},{1,33},{17,49},{33,1},{49,17},{2,34}... | collective-permute-start | bytes 9224 | tf_op jit(solution)/shard_map/ppermute | solution.py:21
  85.8 4.7 %collective-permute-start.26 = (f32[48,128]{1,0:T(8,128)S(1)}, f32[48,128]{1,0:T(8,128)S(1)}, u32[]{:S(2)}, u32[]{:S(2)}) collective-permute-start(f32[48,128]{1,0:T(8,128)S(1)} %fusion.45), channel_id=1, source_target_pairs={{0,128},{64,192},{128,0},{192,64},{1,129},{65,193},{129,1},{193,65... | collective-permute-start | bytes 73736 | tf_op jit(solution)/shard_map/ppermute | solution.py:21
  86.9 3.6 %collective-permute-start.28 = (f32[48,128]{1,0:T(8,128)S(1)}, f32[48,128]{1,0:T(8,128)S(1)}, u32[]{:S(2)}, u32[]{:S(2)}) collective-permute-start(f32[48,128]{1,0:T(8,128)S(1)} %collective-permute-done.27), channel_id=1, source_target_pairs={{0,1},{1,0},{2,3},{3,2},{4,5},{5,4},{6,7},{7,6},{8,9},{9,8},{10,11... | collective-permute-start | bytes 73736 | tf_op jit(solution)/shard_map/ppermute | solution.py:21
  93.3 4.4 %collective-permute-start.31 = (f32[48,128]{1,0:T(8,128)S(1)}, f32[48,128]{1,0:T(8,128)S(1)}, u32[]{:S(2)}, u32[]{:S(2)}) collective-permute-start(f32[48,128]{1,0:T(8,128)S(1)} %add.113.p0), channel_id=1, source_target_pairs={{0,4},{1,13},{2,6},{3,15},{4,8},{5,1},{6,10},{7,3},{8,12},{9,5},{1... | collective-permute-start | bytes 73736 | tf_op jit(solution)/shard_map/ppermute | solution.py:31
  94.3 6.8 %collective-permute-start.30 = (f32[48,128]{1,0:T(8,128)S(1)}, f32[48,128]{1,0:T(8,128)S(1)}, u32[]{:S(2)}, u32[]{:S(2)}) collective-permute-start(f32[48,128]{1,0:T(8,128)S(1)} %add.113.p0), channel_id=1, source_target_pairs={{0,8},{2,10},{4,12},{6,14},{8,0},{10,2},{12,4},{14,6},{1,9},{3,11}... | collective-permute-start | bytes 73736 | tf_op jit(solution)/shard_map/ppermute | solution.py:21
  97.7 4.2 %collective-permute-start.32 = (f32[48,128]{1,0:T(8,128)S(1)}, f32[48,128]{1,0:T(8,128)S(1)}, u32[]{:S(2)}, u32[]{:S(2)}) collective-permute-start(f32[48,128]{1,0:T(8,128)S(1)} %collective-permute-done.31.p2), channel_id=1, source_target_pairs={{0,1},{1,0},{2,3},{3,2},{4,5},{5,4},{6,7},{7,6},{8,9},{9,8},{10,11... | collective-permute-start | bytes 73736 | tf_op jit(solution)/shard_map/ppermute | solution.py:21
  102.5 3.7 %collective-permute-start.34 = (f32[2,128]{1,0:T(2,128)S(1)}, f32[2,128]{1,0:T(2,128)S(1)}, u32[]{:S(2)}, u32[]{:S(2)}) collective-permute-start(f32[2,128]{1,0:T(2,128)S(1)} %get-tuple-element.27.p0), channel_id=1, source_target_pairs={{0,16},{1,49},{16,32},{17,1},{32,48},{33,17},{48,0},{49,33},{2,18}... | collective-permute-start | bytes 3080 | tf_op jit(solution)/shard_map/ppermute | solution.py:31
  105.5 3.9 %collective-permute-start.33 = (f32[2,128]{1,0:T(2,128)S(1)}, f32[2,128]{1,0:T(2,128)S(1)}, u32[]{:S(2)}, u32[]{:S(2)}) collective-permute-start(f32[2,128]{1,0:T(2,128)S(1)} %get-tuple-element.27.p0), channel_id=1, source_target_pairs={{0,32},{16,48},{32,0},{48,16},{1,33},{17,49},{33,1},{49,17},{2,34}... | collective-permute-start | bytes 3080 | tf_op jit(solution)/shard_map/ppermute | solution.py:21
  106.2 3.2 %collective-permute-start.35 = (f32[2,128]{1,0:T(2,128)S(1)}, f32[2,128]{1,0:T(2,128)S(1)}, u32[]{:S(2)}, u32[]{:S(2)}) collective-permute-start(f32[2,128]{1,0:T(2,128)S(1)} %collective-permute-done.34.p2), channel_id=1, source_target_pairs={{0,1},{1,0},{2,3},{3,2},{4,5},{5,4},{6,7},{7,6},{8,9},{9,8},{10,11... | collective-permute-start | bytes 3080 | tf_op jit(solution)/shard_map/ppermute | solution.py:21
  (7 other events, 42.1 us)

commit v2 on v1

--- a/solution.py
+++ b/solution.py
@@ -86,13 +86,14 @@
     return jnp.sum(x, axis=(0, 1), keepdims=True)
 
 
-def rows_kernel(p0, p1, p2, p3, state, stats, pair):
+def rows_kernel(p0, p1, p2, p3, state, stats, same, pair):
     parts = (p0[...] + p1[...]) + (p2[...] + p3[...])
     rows = DECAY * state[...] + (1.0 - DECAY) * (parts[:24] / F)
     here = whole_sum(rows) / D
     inverse = lax.rsqrt(rows / here)
     power = whole_sum(parts[24:] * inverse * inverse)
     stats[...] = rows
+    same[...] = rows
     pair[0:1, :] = jnp.broadcast_to(here, (1, 128))
     pair[1:2, :] = jnp.broadcast_to(power, (1, 128))
 
@@ -102,10 +103,11 @@
         rows_kernel,
         out_shape=[
             jax.ShapeDtypeStruct((24, 128), jnp.float32),
+            jax.ShapeDtypeStruct((24, 128), jnp.float32),
             jax.ShapeDtypeStruct((2, 128), jnp.float32),
         ],
         in_specs=[pl.BlockSpec(memory_space=pltpu.VMEM)] * 5,
-        out_specs=[pl.BlockSpec(memory_space=pltpu.VMEM)] * 2,
+        out_specs=[pl.BlockSpec(memory_space=pltpu.VMEM)] * 3,
         compiler_params=SMALL,
     )(*parts, state)
 
@@ -170,7 +172,7 @@
         return lax.dynamic_slice(out_grad, (start, ((dp + s) % 4) * 768), (size, 768))
 
     near = jnp.stack([shift(units(s, row % 2 * 128, 128), "dp", s) for s in (1, 2, 3)])
-    parcels = [units(0, 0, 256), near, flip(near, "row")]
+    parcels = [units(0, 0, 256), near, apart(near, "row")]
 
     def ring_step(here):
         here = [apart(x, "z") for x in here]
@@ -179,24 +181,22 @@
         return here
 
     def product(h, lo, hi):
-        tokens = jnp.concatenate(halves[h][lo:hi], axis=0)
+        (tokens,) = tie(jnp.concatenate(halves[h][lo:hi], axis=0))
         rows = b[lo * 128 : hi * 128]
         return lax.dot_general(
             tokens, rows, (((0,), (0,)), ((), ())), preferred_element_type=jnp.float32
         )
 
-    here = ring_step(ring_step(here))
-    here, parcels = tie(here, parcels)
+    here = ring_step(ring_step(ring_step(here)))
+    here[1], parcels = tie(here[1], parcels)
+    far = apart(by_core(*here)[0], "z")
     b = order(jnp.stack([z, core, row % 2]), *parcels)
-    here = ring_step(here)
     grads = [product(h, 0, 3) for h in (0, 1)]
-    here[1], grads = tie(here[1], grads)
-    far = apart(by_core(*here)[0], "z")
     grads = [grads[h] + product(h, 3, 7) for h in (0, 1)]
     far, grads = tie(far, grads)
     for half, x in zip(halves, by_core(far, swap(far))):
         half.append(x)
-    grads = [grads[h] + product(h, 7, 8) for h in (0, 1)]
+    (grads,) = tie([grads[h] + product(h, 7, 8) for h in (0, 1)])
 
     col_part = sum(jnp.sum(grad * grad, axis=0) for grad in grads)
     col_sum = total(col_part, "row", 1)
@@ -208,8 +208,8 @@
     parts = parts + swap(parts)
     parts = grouped(parts, "dp", 1)
     parts = parts + flip(parts, "z")
-    row_stats, pair = rows_call(four(parts, "z", 2), row_state.reshape(24, 128))
-    update = update_call(four(pair, "row", 1), row_stats, col_scale.reshape(1, 768), grads)
+    row_stats, rows, pair = rows_call(four(parts, "z", 2), row_state.reshape(24, 128))
+    update = update_call(four(pair, "row", 1), rows, col_scale.reshape(1, 768), grads)
     return (update, row_stats.reshape(3072), col_stats)
 
 

time: 115 us -> 106 us (0.922)
  starting transfers between devices: 62.4 us -> 59.3 us
  matrix products: 10.5 us -> 7.41 us
  waiting for transfers between devices: 26 us -> 23.1 us
  other arithmetic: 5.22 us -> 7.87 us
  local copies, waits for them, and re-layouts: 3.86 us -> 1.81 us
    ppermute x2 -> x1, waiting for transfers between devices: 6.47 us -> 2.66 us  [flip(): return lax.ppermute(x, axis, [(i, i ^ 1) for i in range(SIZE[axis])])]
    dot_general x6, matrix products: 10.5 us -> 7.41 us  [product(): lax.dot_general(tokens, rows, (((0,), (0,)), ((), ())), preferred_element...]
    concatenate x0 -> x4, other arithmetic: none -> 2.36 us  [product(): tokens, = tie(jnp.concatenate(halves[h][lo:hi], axis=0))]
    reduce_sum x2, other arithmetic: 4.29 us -> 2.17 us  [on_device(): parts = [jnp.sum(x * x, axis=1).reshape(12, 128) for x in grads + scaled]]
    ppermute x24, starting transfers between devices: 35.4 us -> 33.5 us  [shift(): return lax.ppermute(x, axis, [(i, (i + step) % n) for i in range(n)])]
    ppermute x10 -> x11, waiting for transfers between devices: 5.86 us -> 7.35 us  [apart(): return lax.ppermute(x, (axis, 'core'), pairs)]
    dynamic_slice x2, local copies, waits for them, and re-layouts: 2.18 us -> 0.83 us  [units(): return lax.dynamic_slice(out_grad, (start, (dp + s) % 4 * 768), (size, 768))]
    ppermute x2 -> x1, starting transfers between devices: 1.39 us -> 0.09 us  [flip(): return lax.ppermute(x, axis, [(i, i ^ 1) for i in range(SIZE[axis])])]
  transfers between devices with their start and end apart: 36 -> 36, of which waited for: 17 -> 16; matrix products, arithmetic and copies ran while one was open for 11% -> 11% of each run, Pallas kernels for 1% -> 1%
where the time goes in v2:
time: 106 us
  starting transfers between devices  59.3 us (56%)
  waiting for transfers between devices  23.1 us (22%)
  other arithmetic  7.87 us (7%)
  matrix products  7.41 us (7%)
  Pallas kernels  5.19 us (5%)
  local copies, waits for them, and re-layouts  1.81 us (2%)
  between operations  1.12 us (1%)
    ppermute x24, starting transfers between devices, shift(): return lax.ppermute(x, axis, [(i, (i + step) % n) for i in range(n)])  33.5 us
    ppermute x11, starting transfers between devices, apart(): return lax.ppermute(x, (axis, 'core'), pairs)  25.7 us
    ppermute x24, waiting for transfers between devices, shift(): return lax.ppermute(x, axis, [(i, (i + step) % n) for i in range(n)])  13.1 us
    dot_general x6, matrix products, product(): lax.dot_general(tokens, rows, (((0,), (0,)), ((), ())), preferred_element...  7.41 us
    ppermute x11, waiting for transfers between devices, apart(): return lax.ppermute(x, (axis, 'core'), pairs)  7.35 us
    pallas_call x1, Pallas kernels, update_call(): pl.pallas_call(update_kernel, out_shape=jax.ShapeDtypeStruct((3072, 768),...  3.87 us
    ppermute x1, waiting for transfers between devices, flip(): return lax.ppermute(x, axis, [(i, i ^ 1) for i in range(SIZE[axis])])  2.66 us
    concatenate x4, other arithmetic, product(): tokens, = tie(jnp.concatenate(halves[h][lo:hi], axis=0))  2.36 us
  transfers between devices with their start and end apart: 36, of which 16 were waited for; matrix products, arithmetic and copies ran while one was open for 11% of the time, Pallas kernels for 1%

profile of v2, /device:TPU:1, one launch (start us, length us, event | category | flops | bytes accessed | tf_op | source)
XLA Modules:
  0.0 105.8 jit_solution(16462960906417558287)
XLA Ops:
  0.6 3.8 %collective-permute-start.1 = (bf16[16,3072]{1,0:T(8,128)(2,1)}, bf16[16,3072]{1,0:T(8,128)(2,1)S(1)}, u32[]{:S(2)}, u32[]{:S(2)}) collective-permute-start(bf16[16,3072]{1,0:T(8,128)(2,1)} %param.4), channel_id=1, source_target_pairs={{0,128},{64,192},{128,0},{192,64},{1,129},{65,193},{129,1},{193,65... | collective-permute-start | bytes 294920 | tf_op jit(solution)/shard_map/ppermute | solution.py:21
  4.9 2.3 %collective-permute-start.2 = (bf16[16,3072]{1,0:T(8,128)(2,1)}, bf16[16,3072]{1,0:T(8,128)(2,1)S(1)}, u32[]{:S(2)}, u32[]{:S(2)}) collective-permute-start(bf16[16,3072]{1,0:T(8,128)(2,1)} %param.4), channel_id=1, source_target_pairs={{0,192},{64,0},{128,64},{192,128},{1,193},{65,1},{129,65},{193,129... | collective-permute-start | bytes 294920 | tf_op jit(solution)/shard_map/ppermute | solution.py:21
  8.1 3.2 %collective-permute-done = bf16[16,3072]{1,0:T(8,128)(2,1)S(1)} collective-permute-done((bf16[16,3072]{1,0:T(8,128)(2,1)}, bf16[16,3072]{1,0:T(8,128)(2,1)S(1)}, u32[]{:S(2)}, u32[]{:S(2)}) %collective-permute-start) | collective-permute-done | bytes 98336 | tf_op jit(solution)/shard_map/ppermute | solution.py:21
  12.3 1.3 %collective-permute-done.3 = bf16[64,3072]{1,0:T(8,128)(2,1)S(1)} collective-permute-done((bf16[64,3072]{1,0:T(8,128)(2,1)S(1)}, bf16[64,3072]{1,0:T(8,128)(2,1)S(1)}, u32[]{:S(2)}, u32[]{:S(2)}) %collective-permute-start.3) | collective-permute-done | bytes 393248 | tf_op jit(solution)/shard_map/ppermute | solution.py:21
  13.8 5.0 %collective-permute-start.7 = (bf16[128,1536]{1,0:T(8,128)(2,1)S(1)}, bf16[128,1536]{1,0:T(8,128)(2,1)S(1)}, u32[]{:S(2)}, u32[]{:S(2)}) collective-permute-start(bf16[128,1536]{1,0:T(8,128)(2,1)S(1)} %get-tuple-element.40), channel_id=1, source_target_pairs={{0,2},{1,15},{2,4},{3,1},{4,6},{5,3},{6,8},{7,5},{8,10},{9,7},{10,... | collective-permute-start | bytes 1179656 | tf_op jit(solution)/shard_map/ppermute | solution.py:31
  20.8 2.3 %collective-permute-start.12 = (bf16[128,768]{1,0:T(8,128)(2,1)}, bf16[128,768]{1,0:T(8,128)(2,1)}, u32[]{:S(2)}, u32[]{:S(2)}) collective-permute-start(bf16[128,768]{1,0:T(8,128)(2,1)} %get-tuple-element.36), channel_id=1, source_target_pairs={{0,192},{64,0},{128,64},{192,128},{1,193},{65,1},{129,65},{193,129... | collective-permute-start | bytes 589832 | tf_op jit(solution)/shard_map/ppermute | solution.py:21
  23.2 1.2 %collective-permute-start.11 = (bf16[128,768]{1,0:T(8,128)(2,1)}, bf16[128,768]{1,0:T(8,128)(2,1)}, u32[]{:S(2)}, u32[]{:S(2)}) collective-permute-start(bf16[128,768]{1,0:T(8,128)(2,1)} %get-tuple-element.37), channel_id=1, source_target_pairs={{0,128},{64,192},{128,0},{192,64},{1,129},{65,193},{129,1},{193,65... | collective-permute-start | bytes 589832 | tf_op jit(solution)/shard_map/ppermute | solution.py:21
  24.4 2.6 %collective-permute-start.8 = (bf16[128,1536]{1,0:T(8,128)(2,1)S(1)}, bf16[128,1536]{1,0:T(8,128)(2,1)}, u32[]{:S(2)}, u32[]{:S(2)}) collective-permute-start(bf16[128,1536]{1,0:T(8,128)(2,1)S(1)} %collective-permute-done.7), channel_id=1, source_target_pairs={{0,2},{1,15},{2,4},{3,1},{4,6},{5,3},{6,8},{7,5},{8,10},{9,7},{10,... | collective-permute-start | bytes 1179656 | tf_op jit(solution)/shard_map/ppermute | solution.py:31
  27.7 3.5 %collective-permute-start.5 = (bf16[128,1536]{1,0:T(8,128)(2,1)S(1)}, bf16[128,1536]{1,0:T(8,128)(2,1)S(1)}, u32[]{:S(2)}, u32[]{:S(2)}) collective-permute-start(bf16[128,1536]{1,0:T(8,128)(2,1)S(1)} %collective-permute-done.4), channel_id=1, source_target_pairs={{0,2},{1,15},{2,4},{3,1},{4,6},{5,3},{6,8},{7,5},{8,10},{9,7},{10,... | collective-permute-start | bytes 1179656 | tf_op jit(solution)/shard_map/ppermute | solution.py:31
  33.4 2.6 %collective-permute-start.13 = (bf16[3,128,768]{2,1,0:T(8,128)(2,1)S(1)}, bf16[3,128,768]{2,1,0:T(8,128)(2,1)S(1)}, u32[]{:S(2)}, u32[]{:S(2)}) collective-permute-start(bf16[3,128,768]{2,1,0:T(8,128)(2,1)S(1)} %pad_maximum_fusion.4.near), channel_id=1, source_target_pairs={{0,16},{1,49},{16,32},{17,1},{32,48},{33,17},{48,0},{49,33},{2,18}... | collective-permute-start | bytes 1769480 | tf_op jit(solution)/shard_map/ppermute | solution.py:31
  36.0 1.9 %collective-permute-start.9 = (bf16[128,1536]{1,0:T(8,128)(2,1)}, bf16[128,1536]{1,0:T(8,128)(2,1)S(1)}, u32[]{:S(2)}, u32[]{:S(2)}) collective-permute-start(bf16[128,1536]{1,0:T(8,128)(2,1)} %collective-permute-done.8), channel_id=1, source_target_pairs={{0,2},{1,15},{2,4},{3,1},{4,6},{5,3},{6,8},{7,5},{8,10},{9,7},{10,... | collective-permute-start | bytes 1179656 | tf_op jit(solution)/shard_map/ppermute | solution.py:31
  38.0 1.3 %collective-permute-start.6 = (bf16[128,1536]{1,0:T(8,128)(2,1)S(1)}, bf16[128,1536]{1,0:T(8,128)(2,1)S(1)}, u32[]{:S(2)}, u32[]{:S(2)}) collective-permute-start(bf16[128,1536]{1,0:T(8,128)(2,1)S(1)} %collective-permute-done.5), channel_id=1, source_target_pairs={{0,2},{1,15},{2,4},{3,1},{4,6},{5,3},{6,8},{7,5},{8,10},{9,7},{10,... | collective-permute-start | bytes 1179656 | tf_op jit(solution)/shard_map/ppermute | solution.py:31
  41.2 1.6 %collective-permute-done.13.far = bf16[3,128,768]{2,1,0:T(8,128)(2,1)S(1)} collective-permute-done((bf16[3,128,768]{2,1,0:T(8,128)(2,1)S(1)}, bf16[3,128,768]{2,1,0:T(8,128)(2,1)S(1)}, u32[]{:S(2)}, u32[]{:S(2)}) %collective-permute-start.13) | collective-permute-done | bytes 589856 | tf_op jit(solution)/shard_map/ppermute | solution.py:31
  43.3 4.2 %collective-permute-done.6 = bf16[128,1536]{1,0:T(8,128)(2,1)S(1)} collective-permute-done((bf16[128,1536]{1,0:T(8,128)(2,1)S(1)}, bf16[128,1536]{1,0:T(8,128)(2,1)S(1)}, u32[]{:S(2)}, u32[]{:S(2)}) %collective-permute-start.6) | collective-permute-done | bytes 393248 | tf_op jit(solution)/shard_map/ppermute | solution.py:31
  47.6 2.7 %collective-permute-start.14 = (bf16[128,1536]{1,0:T(8,128)(2,1)S(1)}, bf16[128,1536]{1,0:T(8,128)(2,1)S(1)}, u32[]{:S(2)}, u32[]{:S(2)}) collective-permute-start(bf16[128,1536]{1,0:T(8,128)(2,1)S(1)} %broadcast_select_fusion.4), channel_id=1, source_target_pairs={{0,2},{1,15},{2,4},{3,1},{4,6},{5,3},{6,8},{7,5},{8,10},{9,7},{10,... | collective-permute-start | bytes 1179656 | tf_op jit(solution)/shard_map/ppermute | solution.py:31
  51.2 1.4 %fusion.2 = f32[1536,768]{1,0:T(8,128)S(1)} fusion(bf16[384,1536]{1,0:T(8,128)(2,1)S(1)} %pad_maximum_fusion.3, bf16[1024,768]{1,0:T(8,128)(2,1)S(1)} %shard_map.67), kind=kOutput, calls=%fused_computation.17 | convolution fusion | flops 905969664 | bytes 6488064 | tf_op jit(solution)/shard_map/dot_general | solution.py:186
  53.2 1.4 %fusion.4 = f32[1536,768]{1,0:T(8,128)S(1)} fusion(bf16[384,1536]{1,0:T(8,128)(2,1)S(1)} %pad_maximum_fusion.2, bf16[1024,768]{1,0:T(8,128)(2,1)S(1)} %shard_map.67), kind=kOutput, calls=%fused_computation.19 | convolution fusion | flops 905969664 | bytes 6488064 | tf_op jit(solution)/shard_map/dot_general | solution.py:186
  55.9 1.5 %convolution_add_fusion = f32[1536,768]{1,0:T(8,128)S(1)} fusion(f32[1536,768]{1,0:T(8,128)S(1)} %fusion.2, bf16[512,1536]{1,0:T(8,128)(2,1)S(1)} %pad_maximum_fusion.1, bf16[1024,768]{1,0:T(8,128)(2,1)S(1)} %shard_map.67), kind=kOutput, calls=%fused_computation.6 | convolution fusion | flops 1209139200 | bytes 11796480 | tf_op jit(solution)/shard_map/dot_general | solution.py:186
  57.3 1.5 %convolution_add_fusion.1 = f32[1536,768]{1,0:T(8,128)S(1)} fusion(f32[1536,768]{1,0:T(8,128)S(1)} %fusion.4, bf16[512,1536]{1,0:T(8,128)(2,1)S(1)} %pad_maximum_fusion, bf16[1024,768]{1,0:T(8,128)(2,1)S(1)} %shard_map.67), kind=kOutput, calls=%fused_computation.7 | convolution fusion | flops 1209139200 | bytes 11796480 | tf_op jit(solution)/shard_map/dot_general | solution.py:186
  59.2 1.7 %collective-permute-done.21 = bf16[128,1536]{1,0:T(8,128)(2,1)S(1)} collective-permute-done((bf16[128,1536]{1,0:T(8,128)(2,1)S(1)}, bf16[128,1536]{1,0:T(8,128)(2,1)S(1)}, u32[]{:S(2)}, u32[]{:S(2)}) %collective-permute-start.21) | collective-permute-done | bytes 393248 | tf_op jit(solution)/shard_map/ppermute | solution.py:21
  67.5 1.7 %collective-permute-done.23 = f32[768]{0:T(1024)S(1)} collective-permute-done((f32[768]{0:T(1024)S(1)}, f32[768]{0:T(1024)S(1)}, u32[]{:S(2)}, u32[]{:S(2)}) %collective-permute-start.23) | collective-permute-done | bytes 3104 | tf_op jit(solution)/shard_map/ppermute | solution.py:21
  69.3 1.2 %collective-permute-done.22 = f32[768]{0:T(1024)S(1)} collective-permute-done((f32[768]{0:T(1024)S(1)}, f32[768]{0:T(1024)S(1)}, u32[]{:S(2)}, u32[]{:S(2)}) %collective-permute-start.22) | collective-permute-done | bytes 3104 | tf_op jit(solution)/shard_map/ppermute | solution.py:21
  72.1 1.9 %collective-permute-start.25 = (f32[48,128]{1,0:T(8,128)S(1)}, f32[48,128]{1,0:T(8,128)S(1)}, u32[]{:S(2)}, u32[]{:S(2)}) collective-permute-start(f32[48,128]{1,0:T(8,128)S(1)} %pad_maximum_fusion.6), channel_id=1, source_target_pairs={{0,1},{1,0},{2,3},{3,2},{4,5},{5,4},{6,7},{7,6},{8,9},{9,8},{10,11... | collective-permute-start | bytes 73736 | tf_op jit(solution)/shard_map/ppermute | solution.py:21
  74.9 2.2 %collective-permute-start.27 = (f32[48,128]{1,0:T(8,128)S(1)}, f32[48,128]{1,0:T(8,128)S(1)}, u32[]{:S(2)}, u32[]{:S(2)}) collective-permute-start(f32[48,128]{1,0:T(8,128)S(1)} %fusion.19), channel_id=1, source_target_pairs={{0,64},{1,193},{64,128},{65,1},{128,192},{129,65},{192,0},{193,129... | collective-permute-start | bytes 73736 | tf_op jit(solution)/shard_map/ppermute | solution.py:31
  78.3 2.1 %collective-permute-start.28 = (f32[48,128]{1,0:T(8,128)S(1)}, f32[48,128]{1,0:T(8,128)S(1)}, u32[]{:S(2)}, u32[]{:S(2)}) collective-permute-start(f32[48,128]{1,0:T(8,128)S(1)} %collective-permute-done.27), channel_id=1, source_target_pairs={{0,1},{1,0},{2,3},{3,2},{4,5},{5,4},{6,7},{7,6},{8,9},{9,8},{10,11... | collective-permute-start | bytes 73736 | tf_op jit(solution)/shard_map/ppermute | solution.py:21
  81.5 2.7 %collective-permute-done.29 = f32[48,128]{1,0:T(8,128)S(1)} collective-permute-done((f32[48,128]{1,0:T(8,128)S(1)}, f32[48,128]{1,0:T(8,128)S(1)}, u32[]{:S(2)}, u32[]{:S(2)}) %collective-permute-start.29) | collective-permute-done | bytes 24608 | tf_op jit(solution)/shard_map/ppermute | solution.py:39
  84.1 1.4 %collective-permute-start.31 = (f32[48,128]{1,0:T(8,128)S(1)}, f32[48,128]{1,0:T(8,128)S(1)}, u32[]{:S(2)}, u32[]{:S(2)}) collective-permute-start(f32[48,128]{1,0:T(8,128)S(1)} %add.113.p0), channel_id=1, source_target_pairs={{0,4},{1,13},{2,6},{3,15},{4,8},{5,1},{6,10},{7,3},{8,12},{9,5},{1... | collective-permute-start | bytes 73736 | tf_op jit(solution)/shard_map/ppermute | solution.py:31
  85.6 4.7 %collective-permute-start.30 = (f32[48,128]{1,0:T(8,128)S(1)}, f32[48,128]{1,0:T(8,128)S(1)}, u32[]{:S(2)}, u32[]{:S(2)}) collective-permute-start(f32[48,128]{1,0:T(8,128)S(1)} %add.113.p0), channel_id=1, source_target_pairs={{0,8},{2,10},{4,12},{6,14},{8,0},{10,2},{12,4},{14,6},{1,9},{3,11}... | collective-permute-start | bytes 73736 | tf_op jit(solution)/shard_map/ppermute | solution.py:21
  90.3 2.3 %collective-permute-start.32 = (f32[48,128]{1,0:T(8,128)S(1)}, f32[48,128]{1,0:T(8,128)S(1)}, u32[]{:S(2)}, u32[]{:S(2)}) collective-permute-start(f32[48,128]{1,0:T(8,128)S(1)} %collective-permute-done.31.p2), channel_id=1, source_target_pairs={{0,1},{1,0},{2,3},{3,2},{4,5},{5,4},{6,7},{7,6},{8,9},{9,8},{10,11... | collective-permute-start | bytes 73736 | tf_op jit(solution)/shard_map/ppermute | solution.py:21
  94.0 1.7 %collective-permute-start.34 = (f32[2,128]{1,0:T(2,128)S(1)}, f32[2,128]{1,0:T(2,128)S(1)}, u32[]{:S(2)}, u32[]{:S(2)}) collective-permute-start(f32[2,128]{1,0:T(2,128)S(1)} %get-tuple-element.24.p0), channel_id=1, source_target_pairs={{0,16},{1,49},{16,32},{17,1},{32,48},{33,17},{48,0},{49,33},{2,18}... | collective-permute-start | bytes 3080 | tf_op jit(solution)/shard_map/ppermute | solution.py:31
  96.5 4.5 %collective-permute-start.35 = (f32[2,128]{1,0:T(2,128)S(1)}, f32[2,128]{1,0:T(2,128)S(1)}, u32[]{:S(2)}, u32[]{:S(2)}) collective-permute-start(f32[2,128]{1,0:T(2,128)S(1)} %collective-permute-done.34.p2), channel_id=1, source_target_pairs={{0,1},{1,0},{2,3},{3,2},{4,5},{5,4},{6,7},{7,6},{8,9},{9,8},{10,11... | collective-permute-start | bytes 3080 | tf_op jit(solution)/shard_map/ppermute | solution.py:21
  101.7 3.9 %shard_map.69 = f32[3072,768]{1,0:T(8,128)} custom-call(f32[2,128]{1,0:T(2,128)S(1)} %get-tuple-element.24.p0, f32[2,128]{1,0:T(2,128)S(1)} %collective-permute-done.33.p1, f32[2,128]{1,0:T(2,128)S(1)} %collective-permute-done.34.p2, f32[2,128]{1,0:T(2,128)S(1)} %collective-permute-done.35.p3, f32[24,128]{1,0:T(8,128)S(1)} %get-tuple-element.25.stats, ...), custom_call_target="tpu_custom_call" | custom-call | tf_op jit(solution)/shard_map/pallas_call | solution.py:143
  (82 shorter events, 27.2 us)
Async XLA Ops:
  0.6 10.7 %collective-permute-start.1 = (bf16[16,3072]{1,0:T(8,128)(2,1)}, bf16[16,3072]{1,0:T(8,128)(2,1)S(1)}, u32[]{:S(2)}, u32[]{:S(2)}) collective-permute-start(bf16[16,3072]{1,0:T(8,128)(2,1)} %param.4), channel_id=1, source_target_pairs={{0,128},{64,192},{128,0},{192,64},{1,129},{65,193},{129,1},{193,65... | collective-permute-start | bytes 294920 | tf_op jit(solution)/shard_map/ppermute | solution.py:21
  4.5 6.9 %collective-permute-start = (bf16[16,3072]{1,0:T(8,128)(2,1)}, bf16[16,3072]{1,0:T(8,128)(2,1)S(1)}, u32[]{:S(2)}, u32[]{:S(2)}) collective-permute-start(bf16[16,3072]{1,0:T(8,128)(2,1)} %param.4), channel_id=1, source_target_pairs={{0,64},{64,128},{128,192},{192,0},{1,65},{65,129},{129,193},{193,1... | collective-permute-start | bytes 294920 | tf_op jit(solution)/shard_map/ppermute | solution.py:21
  4.9 6.5 %collective-permute-start.2 = (bf16[16,3072]{1,0:T(8,128)(2,1)}, bf16[16,3072]{1,0:T(8,128)(2,1)S(1)}, u32[]{:S(2)}, u32[]{:S(2)}) collective-permute-start(bf16[16,3072]{1,0:T(8,128)(2,1)} %param.4), channel_id=1, source_target_pairs={{0,192},{64,0},{128,64},{192,128},{1,193},{65,1},{129,65},{193,129... | collective-permute-start | bytes 294920 | tf_op jit(solution)/shard_map/ppermute | solution.py:21
  13.8 10.6 %collective-permute-start.7 = (bf16[128,1536]{1,0:T(8,128)(2,1)S(1)}, bf16[128,1536]{1,0:T(8,128)(2,1)S(1)}, u32[]{:S(2)}, u32[]{:S(2)}) collective-permute-start(bf16[128,1536]{1,0:T(8,128)(2,1)S(1)} %get-tuple-element.40), channel_id=1, source_target_pairs={{0,2},{1,15},{2,4},{3,1},{4,6},{5,3},{6,8},{7,5},{8,10},{9,7},{10,... | collective-permute-start | bytes 1179656 | tf_op jit(solution)/shard_map/ppermute | solution.py:31
  18.7 8.9 %collective-permute-start.4 = (bf16[128,1536]{1,0:T(8,128)(2,1)S(1)}, bf16[128,1536]{1,0:T(8,128)(2,1)S(1)}, u32[]{:S(2)}, u32[]{:S(2)}) collective-permute-start(bf16[128,1536]{1,0:T(8,128)(2,1)S(1)} %get-tuple-element.41), channel_id=1, source_target_pairs={{0,2},{1,15},{2,4},{3,1},{4,6},{5,3},{6,8},{7,5},{8,10},{9,7},{10,... | collective-permute-start | bytes 1179656 | tf_op jit(solution)/shard_map/ppermute | solution.py:31
  20.3 10.9 %collective-permute-start.10 = (bf16[128,768]{1,0:T(8,128)(2,1)S(1)}, bf16[128,768]{1,0:T(8,128)(2,1)}, u32[]{:S(2)}, u32[]{:S(2)}) collective-permute-start(bf16[128,768]{1,0:T(8,128)(2,1)S(1)} %get-tuple-element.35), channel_id=1, source_target_pairs={{0,64},{64,128},{128,192},{192,0},{1,65},{65,129},{129,193},{193,1... | collective-permute-start | bytes 589832 | tf_op jit(solution)/shard_map/ppermute | solution.py:21
  20.8 10.4 %collective-permute-start.12 = (bf16[128,768]{1,0:T(8,128)(2,1)}, bf16[128,768]{1,0:T(8,128)(2,1)}, u32[]{:S(2)}, u32[]{:S(2)}) collective-permute-start(bf16[128,768]{1,0:T(8,128)(2,1)} %get-tuple-element.36), channel_id=1, source_target_pairs={{0,192},{64,0},{128,64},{192,128},{1,193},{65,1},{129,65},{193,129... | collective-permute-start | bytes 589832 | tf_op jit(solution)/shard_map/ppermute | solution.py:21
  23.2 9.0 %collective-permute-start.11 = (bf16[128,768]{1,0:T(8,128)(2,1)}, bf16[128,768]{1,0:T(8,128)(2,1)}, u32[]{:S(2)}, u32[]{:S(2)}) collective-permute-start(bf16[128,768]{1,0:T(8,128)(2,1)} %get-tuple-element.37), channel_id=1, source_target_pairs={{0,128},{64,192},{128,0},{192,64},{1,129},{65,193},{129,1},{193,65... | collective-permute-start | bytes 589832 | tf_op jit(solution)/shard_map/ppermute | solution.py:21
  24.4 11.7 %collective-permute-start.8 = (bf16[128,1536]{1,0:T(8,128)(2,1)S(1)}, bf16[128,1536]{1,0:T(8,128)(2,1)}, u32[]{:S(2)}, u32[]{:S(2)}) collective-permute-start(bf16[128,1536]{1,0:T(8,128)(2,1)S(1)} %collective-permute-done.7), channel_id=1, source_target_pairs={{0,2},{1,15},{2,4},{3,1},{4,6},{5,3},{6,8},{7,5},{8,10},{9,7},{10,... | collective-permute-start | bytes 1179656 | tf_op jit(solution)/shard_map/ppermute | solution.py:31
  27.7 10.3 %collective-permute-start.5 = (bf16[128,1536]{1,0:T(8,128)(2,1)S(1)}, bf16[128,1536]{1,0:T(8,128)(2,1)S(1)}, u32[]{:S(2)}, u32[]{:S(2)}) collective-permute-start(bf16[128,1536]{1,0:T(8,128)(2,1)S(1)} %collective-permute-done.4), channel_id=1, source_target_pairs={{0,2},{1,15},{2,4},{3,1},{4,6},{5,3},{6,8},{7,5},{8,10},{9,7},{10,... | collective-permute-start | bytes 1179656 | tf_op jit(solution)/shard_map/ppermute | solution.py:31
  31.2 8.0 %collective-permute-start.18 = (bf16[128,1536]{1,0:T(8,128)(2,1)S(1)}, bf16[128,1536]{1,0:T(8,128)(2,1)}, u32[]{:S(2)}, u32[]{:S(2)}) collective-permute-start(bf16[128,1536]{1,0:T(8,128)(2,1)S(1)} %collective-permute-done.7), channel_id=1, source_target_pairs={{0,1},{1,0},{2,3},{3,2},{4,5},{5,4},{6,7},{7,6},{8,9},{9,8},{10,11... | collective-permute-start | bytes 1179656 | tf_op jit(solution)/shard_map/ppermute | solution.py:21
  31.2 9.1 %collective-permute-start.15 = (bf16[128,1536]{1,0:T(8,128)(2,1)S(1)}, bf16[128,1536]{1,0:T(8,128)(2,1)S(1)}, u32[]{:S(2)}, u32[]{:S(2)}) collective-permute-start(bf16[128,1536]{1,0:T(8,128)(2,1)S(1)} %collective-permute-done.4), channel_id=1, source_target_pairs={{0,1},{1,0},{2,3},{3,2},{4,5},{5,4},{6,7},{7,6},{8,9},{9,8},{10,11... | collective-permute-start | bytes 1179656 | tf_op jit(solution)/shard_map/ppermute | solution.py:21
  33.4 9.4 %collective-permute-start.13 = (bf16[3,128,768]{2,1,0:T(8,128)(2,1)S(1)}, bf16[3,128,768]{2,1,0:T(8,128)(2,1)S(1)}, u32[]{:S(2)}, u32[]{:S(2)}) collective-permute-start(bf16[3,128,768]{2,1,0:T(8,128)(2,1)S(1)} %pad_maximum_fusion.4.near), channel_id=1, source_target_pairs={{0,16},{1,49},{16,32},{17,1},{32,48},{33,17},{48,0},{49,33},{2,18}... | collective-permute-start | bytes 1769480 | tf_op jit(solution)/shard_map/ppermute | solution.py:31
  36.0 7.3 %collective-permute-start.9 = (bf16[128,1536]{1,0:T(8,128)(2,1)}, bf16[128,1536]{1,0:T(8,128)(2,1)S(1)}, u32[]{:S(2)}, u32[]{:S(2)}) collective-permute-start(bf16[128,1536]{1,0:T(8,128)(2,1)} %collective-permute-done.8), channel_id=1, source_target_pairs={{0,2},{1,15},{2,4},{3,1},{4,6},{5,3},{6,8},{7,5},{8,10},{9,7},{10,... | collective-permute-start | bytes 1179656 | tf_op jit(solution)/shard_map/ppermute | solution.py:31
  38.0 9.6 %collective-permute-start.6 = (bf16[128,1536]{1,0:T(8,128)(2,1)S(1)}, bf16[128,1536]{1,0:T(8,128)(2,1)S(1)}, u32[]{:S(2)}, u32[]{:S(2)}) collective-permute-start(bf16[128,1536]{1,0:T(8,128)(2,1)S(1)} %collective-permute-done.5), channel_id=1, source_target_pairs={{0,2},{1,15},{2,4},{3,1},{4,6},{5,3},{6,8},{7,5},{8,10},{9,7},{10,... | collective-permute-start | bytes 1179656 | tf_op jit(solution)/shard_map/ppermute | solution.py:31
  40.4 14.2 %collective-permute-start.19 = (bf16[128,1536]{1,0:T(8,128)(2,1)}, bf16[128,1536]{1,0:T(8,128)(2,1)S(1)}, u32[]{:S(2)}, u32[]{:S(2)}) collective-permute-start(bf16[128,1536]{1,0:T(8,128)(2,1)} %collective-permute-done.8), channel_id=1, source_target_pairs={{0,1},{1,0},{2,3},{3,2},{4,5},{5,4},{6,7},{7,6},{8,9},{9,8},{10,11... | collective-permute-start | bytes 1179656 | tf_op jit(solution)/shard_map/ppermute | solution.py:21
  40.7 15.0 %collective-permute-start.16 = (bf16[128,1536]{1,0:T(8,128)(2,1)S(1)}, bf16[128,1536]{1,0:T(8,128)(2,1)S(1)}, u32[]{:S(2)}, u32[]{:S(2)}) collective-permute-start(bf16[128,1536]{1,0:T(8,128)(2,1)S(1)} %collective-permute-done.5), channel_id=1, source_target_pairs={{0,1},{1,0},{2,3},{3,2},{4,5},{5,4},{6,7},{7,6},{8,9},{9,8},{10,11... | collective-permute-start | bytes 1179656 | tf_op jit(solution)/shard_map/ppermute | solution.py:21
  47.6 11.2 %collective-permute-start.14 = (bf16[128,1536]{1,0:T(8,128)(2,1)S(1)}, bf16[128,1536]{1,0:T(8,128)(2,1)S(1)}, u32[]{:S(2)}, u32[]{:S(2)}) collective-permute-start(bf16[128,1536]{1,0:T(8,128)(2,1)S(1)} %broadcast_select_fusion.4), channel_id=1, source_target_pairs={{0,2},{1,15},{2,4},{3,1},{4,6},{5,3},{6,8},{7,5},{8,10},{9,7},{10,... | collective-permute-start | bytes 1179656 | tf_op jit(solution)/shard_map/ppermute | solution.py:31
  51.1 3.6 %collective-permute-start.20 = (bf16[128,1536]{1,0:T(8,128)(2,1)S(1)}, bf16[128,1536]{1,0:T(8,128)(2,1)S(1)}, u32[]{:S(2)}, u32[]{:S(2)}) collective-permute-start(bf16[128,1536]{1,0:T(8,128)(2,1)S(1)} %collective-permute-done.9), channel_id=1, source_target_pairs={{0,1},{1,0},{2,3},{3,2},{4,5},{5,4},{6,7},{7,6},{8,9},{9,8},{10,11... | collective-permute-start | bytes 1179656 | tf_op jit(solution)/shard_map/ppermute | solution.py:21
  52.6 3.1 %collective-permute-start.17 = (bf16[128,1536]{1,0:T(8,128)(2,1)S(1)}, bf16[128,1536]{1,0:T(8,128)(2,1)S(1)}, u32[]{:S(2)}, u32[]{:S(2)}) collective-permute-start(bf16[128,1536]{1,0:T(8,128)(2,1)S(1)} %collective-permute-done.6), channel_id=1, source_target_pairs={{0,1},{1,0},{2,3},{3,2},{4,5},{5,4},{6,7},{7,6},{8,9},{9,8},{10,11... | collective-permute-start | bytes 1179656 | tf_op jit(solution)/shard_map/ppermute | solution.py:21
  65.6 3.7 %collective-permute-start.23 = (f32[768]{0:T(1024)S(1)}, f32[768]{0:T(1024)S(1)}, u32[]{:S(2)}, u32[]{:S(2)}) collective-permute-start(f32[768]{0:T(1024)S(1)} %add.104), channel_id=1, source_target_pairs={{0,16},{16,32},{32,48},{48,0},{1,17},{17,33},{33,49},{49,1},{2,18}... | collective-permute-start | bytes 9224 | tf_op jit(solution)/shard_map/ppermute | solution.py:21
  66.5 4.0 %collective-permute-start.22 = (f32[768]{0:T(1024)S(1)}, f32[768]{0:T(1024)S(1)}, u32[]{:S(2)}, u32[]{:S(2)}) collective-permute-start(f32[768]{0:T(1024)S(1)} %add.104), channel_id=1, source_target_pairs={{0,32},{16,48},{32,0},{48,16},{1,33},{17,49},{33,1},{49,17},{2,34}... | collective-permute-start | bytes 9224 | tf_op jit(solution)/shard_map/ppermute | solution.py:21
  72.1 2.8 %collective-permute-start.25 = (f32[48,128]{1,0:T(8,128)S(1)}, f32[48,128]{1,0:T(8,128)S(1)}, u32[]{:S(2)}, u32[]{:S(2)}) collective-permute-start(f32[48,128]{1,0:T(8,128)S(1)} %pad_maximum_fusion.6), channel_id=1, source_target_pairs={{0,1},{1,0},{2,3},{3,2},{4,5},{5,4},{6,7},{7,6},{8,9},{9,8},{10,11... | collective-permute-start | bytes 73736 | tf_op jit(solution)/shard_map/ppermute | solution.py:21
  74.9 3.3 %collective-permute-start.27 = (f32[48,128]{1,0:T(8,128)S(1)}, f32[48,128]{1,0:T(8,128)S(1)}, u32[]{:S(2)}, u32[]{:S(2)}) collective-permute-start(f32[48,128]{1,0:T(8,128)S(1)} %fusion.19), channel_id=1, source_target_pairs={{0,64},{1,193},{64,128},{65,1},{128,192},{129,65},{192,0},{193,129... | collective-permute-start | bytes 73736 | tf_op jit(solution)/shard_map/ppermute | solution.py:31
  77.2 4.2 %collective-permute-start.26 = (f32[48,128]{1,0:T(8,128)S(1)}, f32[48,128]{1,0:T(8,128)S(1)}, u32[]{:S(2)}, u32[]{:S(2)}) collective-permute-start(f32[48,128]{1,0:T(8,128)S(1)} %fusion.19), channel_id=1, source_target_pairs={{0,128},{64,192},{128,0},{192,64},{1,129},{65,193},{129,1},{193,65... | collective-permute-start | bytes 73736 | tf_op jit(solution)/shard_map/ppermute | solution.py:21
  78.3 3.1 %collective-permute-start.28 = (f32[48,128]{1,0:T(8,128)S(1)}, f32[48,128]{1,0:T(8,128)S(1)}, u32[]{:S(2)}, u32[]{:S(2)}) collective-permute-start(f32[48,128]{1,0:T(8,128)S(1)} %collective-permute-done.27), channel_id=1, source_target_pairs={{0,1},{1,0},{2,3},{3,2},{4,5},{5,4},{6,7},{7,6},{8,9},{9,8},{10,11... | collective-permute-start | bytes 73736 | tf_op jit(solution)/shard_map/ppermute | solution.py:21
  81.4 2.8 %collective-permute-start.29 = (f32[48,128]{1,0:T(8,128)S(1)}, f32[48,128]{1,0:T(8,128)S(1)}, u32[]{:S(2)}, u32[]{:S(2)}) collective-permute-start(f32[48,128]{1,0:T(8,128)S(1)} %add_add_fusion), channel_id=1, source_target_pairs={{0,2},{2,0},{4,6},{6,4},{8,10},{10,8},{12,14},{14,12},{1,3},{3,1},... | collective-permute-start | bytes 73736 | tf_op jit(solution)/shard_map/ppermute | solution.py:39
  84.1 6.1 %collective-permute-start.31 = (f32[48,128]{1,0:T(8,128)S(1)}, f32[48,128]{1,0:T(8,128)S(1)}, u32[]{:S(2)}, u32[]{:S(2)}) collective-permute-start(f32[48,128]{1,0:T(8,128)S(1)} %add.113.p0), channel_id=1, source_target_pairs={{0,4},{1,13},{2,6},{3,15},{4,8},{5,1},{6,10},{7,3},{8,12},{9,5},{1... | collective-permute-start | bytes 73736 | tf_op jit(solution)/shard_map/ppermute | solution.py:31
  85.6 7.0 %collective-permute-start.30 = (f32[48,128]{1,0:T(8,128)S(1)}, f32[48,128]{1,0:T(8,128)S(1)}, u32[]{:S(2)}, u32[]{:S(2)}) collective-permute-start(f32[48,128]{1,0:T(8,128)S(1)} %add.113.p0), channel_id=1, source_target_pairs={{0,8},{2,10},{4,12},{6,14},{8,0},{10,2},{12,4},{14,6},{1,9},{3,11}... | collective-permute-start | bytes 73736 | tf_op jit(solution)/shard_map/ppermute | solution.py:21
  90.3 3.1 %collective-permute-start.32 = (f32[48,128]{1,0:T(8,128)S(1)}, f32[48,128]{1,0:T(8,128)S(1)}, u32[]{:S(2)}, u32[]{:S(2)}) collective-permute-start(f32[48,128]{1,0:T(8,128)S(1)} %collective-permute-done.31.p2), channel_id=1, source_target_pairs={{0,1},{1,0},{2,3},{3,2},{4,5},{5,4},{6,7},{7,6},{8,9},{9,8},{10,11... | collective-permute-start | bytes 73736 | tf_op jit(solution)/shard_map/ppermute | solution.py:21
  95.7 5.2 %collective-permute-start.33 = (f32[2,128]{1,0:T(2,128)S(1)}, f32[2,128]{1,0:T(2,128)S(1)}, u32[]{:S(2)}, u32[]{:S(2)}) collective-permute-start(f32[2,128]{1,0:T(2,128)S(1)} %get-tuple-element.24.p0), channel_id=1, source_target_pairs={{0,32},{16,48},{32,0},{48,16},{1,33},{17,49},{33,1},{49,17},{2,34}... | collective-permute-start | bytes 3080 | tf_op jit(solution)/shard_map/ppermute | solution.py:21
  96.5 5.3 %collective-permute-start.35 = (f32[2,128]{1,0:T(2,128)S(1)}, f32[2,128]{1,0:T(2,128)S(1)}, u32[]{:S(2)}, u32[]{:S(2)}) collective-permute-start(f32[2,128]{1,0:T(2,128)S(1)} %collective-permute-done.34.p2), channel_id=1, source_target_pairs={{0,1},{1,0},{2,3},{3,2},{4,5},{5,4},{6,7},{7,6},{8,9},{9,8},{10,11... | collective-permute-start | bytes 3080 | tf_op jit(solution)/shard_map/ppermute | solution.py:21
  (7 other events, 57.1 us)

commit v3 on v2

--- a/solution.py
+++ b/solution.py
@@ -112,45 +112,46 @@
     )(*parts, state)
 
 
-def update_kernel(p0, p1, p2, p3, stats, scale, grad0, grad1, out, buffer, sems):
+def update_kernel(core, p0, p1, p2, p3, stats, scale, grad0, grad1, out, scales, buffer, sems):
     shares = [p[...] for p in (p0, p1, p2, p3)]
     row_mean = (shares[0][0:1] + shares[1][0:1]) + (shares[2][0:1] + shares[3][0:1])
     powers = [p[1:2] * (row_mean / p[0:1]) for p in shares]
     power_sum = (powers[0] + powers[1]) + (powers[2] + powers[3])
     clip_factor = jnp.maximum(1.0, jnp.sqrt(power_sum / (D * F)) / CLIP)
-    row_scale = lax.rsqrt(stats[...] / row_mean) / clip_factor
+    scales[...] = lax.rsqrt(stats[...] / row_mean) / clip_factor
     copies = [None] * 12
     for k in range(12):
-        grad = (grad0, grad1)[k // 6]
+        grad, half = ((grad0, core[0]), (grad1, 1 - core[0]))[k // 6]
         if k >= 4:
             copies[k - 4].wait()
         for j in range(2):
-            row = row_scale[2 * k + j : 2 * k + j + 1, :]
+            row = scales[pl.ds(half * 12 + (k % 6) * 2 + j, 1), :]
             down = jnp.transpose(jnp.broadcast_to(row, (128, 128)))
             start = (k % 6) * 256 + j * 128
             for c in range(0, 768, 128):
                 value = grad[start : start + 128, c : c + 128] * down
                 buffer[k % 4, j * 128 : (j + 1) * 128, c : c + 128] = value * scale[:, c : c + 128]
-        copies[k] = pltpu.make_async_copy(
-            buffer.at[k % 4], out.at[pl.ds(k * 256, 256), :], sems.at[k % 4]
-        )
+        rows = pl.ds(pl.multiple_of(half * 1536 + (k % 6) * 256, 256), 256)
+        copies[k] = pltpu.make_async_copy(buffer.at[k % 4], out.at[rows, :], sems.at[k % 4])
         copies[k].start()
     for k in range(8, 12):
         copies[k].wait()
 
 
-def update_call(shares, stats, scale, grads):
+def update_call(core, shares, stats, scale, grads):
     return pl.pallas_call(
         update_kernel,
         out_shape=jax.ShapeDtypeStruct((3072, 768), jnp.float32),
-        in_specs=[pl.BlockSpec(memory_space=pltpu.VMEM)] * 8,
+        in_specs=[pl.BlockSpec(memory_space=pltpu.SMEM)]
+        + [pl.BlockSpec(memory_space=pltpu.VMEM)] * 8,
         out_specs=pl.BlockSpec(memory_space=pl.ANY),
         scratch_shapes=[
+            pltpu.VMEM((24, 128), jnp.float32),
             pltpu.VMEM((4, 256, 768), jnp.float32),
             pltpu.SemaphoreType.DMA((4,)),
         ],
         compiler_params=SMALL,
-    )(*shares, stats, scale, *grads)
+    )(core.reshape(1), *shares, stats, scale, *grads)
 
 
 def on_device(tokens_in, out_grad, row_state, col_state):
@@ -165,7 +166,7 @@
 
     own = jnp.concatenate(direct(tokens_in, "dp"), axis=0)
     whole = jnp.concatenate(by_core(own, swap(own)), axis=0)
-    here = [whole[:, :1536], whole[:, 1536:]]
+    here = list(by_core(whole[:, :1536], whole[:, 1536:]))
     halves = [[x] for x in here]
 
     def units(s, start, size):
@@ -176,8 +177,8 @@
 
     def ring_step(here):
         here = [apart(x, "z") for x in here]
-        for half, x in zip(halves, here):
-            half += [x, swap(x)]
+        halves[0] += [here[0], swap(here[1])]
+        halves[1] += [here[1], swap(here[0])]
         return here
 
     def product(h, lo, hi):
@@ -188,14 +189,14 @@
         )
 
     here = ring_step(ring_step(ring_step(here)))
-    here[1], parcels = tie(here[1], parcels)
-    far = apart(by_core(*here)[0], "z")
+    here[0], parcels = tie(here[0], parcels)
+    far = apart(here[0], "z")
     b = order(jnp.stack([z, core, row % 2]), *parcels)
     grads = [product(h, 0, 3) for h in (0, 1)]
     grads = [grads[h] + product(h, 3, 7) for h in (0, 1)]
-    far, grads = tie(far, grads)
-    for half, x in zip(halves, by_core(far, swap(far))):
-        half.append(x)
+    far, grads[0] = tie(far, grads[0])
+    halves[0].append(far)
+    halves[1].append(swap(far))
     (grads,) = tie([grads[h] + product(h, 7, 8) for h in (0, 1)])
 
     col_part = sum(jnp.sum(grad * grad, axis=0) for grad in grads)
@@ -204,12 +205,12 @@
     col_scale = lax.rsqrt(col_stats)
     scaled = [grad * col_scale[None, :] for grad in grads]
     parts = [jnp.sum(x * x, axis=1).reshape(12, 128) for x in grads + scaled]
-    parts = jnp.concatenate(parts, axis=0)
+    parts = jnp.concatenate([*by_core(*parts[:2]), *by_core(*parts[2:])], axis=0)
     parts = parts + swap(parts)
     parts = grouped(parts, "dp", 1)
     parts = parts + flip(parts, "z")
     row_stats, rows, pair = rows_call(four(parts, "z", 2), row_state.reshape(24, 128))
-    update = update_call(four(pair, "row", 1), rows, col_scale.reshape(1, 768), grads)
+    update = update_call(core, four(pair, "row", 1), rows, col_scale.reshape(1, 768), grads)
     return (update, row_stats.reshape(3072), col_stats)
 
 

time: 106 us -> 104 us (0.981)
  other arithmetic: 7.87 us -> 6.63 us
  starting transfers between devices: 59.3 us -> 58.1 us
    ppermute x24, starting transfers between devices: 33.5 us -> 31.2 us  [shift(): return lax.ppermute(x, axis, [(i, (i + step) % n) for i in range(n)])]
    add x2 -> x0, other arithmetic: 1.19 us -> none  [on_device(): grads, = tie([grads[h] + product(h, 7, 8) for h in (0, 1)])]
  transfers between devices with their start and end apart: 36 -> 36, of which waited for: 16 -> 16; matrix products, arithmetic and copies ran while one was open for 11% -> 10% of each run, Pallas kernels for 1% -> 1%
where the time goes in v3:
time: 104 us
  starting transfers between devices  58.1 us (56%)
  waiting for transfers between devices  23.1 us (22%)
  matrix products  7.68 us (7%)
  other arithmetic  6.63 us (6%)
  Pallas kernels  5.19 us (5%)
  local copies, waits for them, and re-layouts  1.81 us (2%)
  between operations  1.09 us (1%)
    ppermute x24, starting transfers between devices, shift(): return lax.ppermute(x, axis, [(i, (i + step) % n) for i in range(n)])  31.2 us
    ppermute x11, starting transfers between devices, apart(): return lax.ppermute(x, (axis, 'core'), pairs)  26.8 us
    ppermute x24, waiting for transfers between devices, shift(): return lax.ppermute(x, axis, [(i, (i + step) % n) for i in range(n)])  12.2 us
    ppermute x11, waiting for transfers between devices, apart(): return lax.ppermute(x, (axis, 'core'), pairs)  8.24 us
    dot_general x6, matrix products, product(): lax.dot_general(tokens, rows, (((0,), (0,)), ((), ())), preferred_element...  7.68 us
    pallas_call x1, Pallas kernels, update_call(): pl.pallas_call(update_kernel, out_shape=jax.ShapeDtypeStruct((3072, 768),...  3.88 us
    ppermute x1, waiting for transfers between devices, flip(): return lax.ppermute(x, axis, [(i, i ^ 1) for i in range(SIZE[axis])])  2.66 us
    concatenate x4, other arithmetic, product(): tokens, = tie(jnp.concatenate(halves[h][lo:hi], axis=0))  2.36 us
  transfers between devices with their start and end apart: 36, of which 16 were waited for; matrix products, arithmetic and copies ran while one was open for 10% of the time, Pallas kernels for 1%

profile of v3, /device:TPU:1, one launch (start us, length us, event | category | flops | bytes accessed | tf_op | source)
XLA Modules:
  0.0 103.6 jit_solution(5077399791930739963)
XLA Ops:
  0.6 3.8 %collective-permute-start.1 = (bf16[16,3072]{1,0:T(8,128)(2,1)}, bf16[16,3072]{1,0:T(8,128)(2,1)S(1)}, u32[]{:S(2)}, u32[]{:S(2)}) collective-permute-start(bf16[16,3072]{1,0:T(8,128)(2,1)} %param.4), channel_id=1, source_target_pairs={{0,128},{64,192},{128,0},{192,64},{1,129},{65,193},{129,1},{193,65... | collective-permute-start | bytes 294920 | tf_op jit(solution)/shard_map/ppermute | solution.py:21
  4.9 2.3 %collective-permute-start.2 = (bf16[16,3072]{1,0:T(8,128)(2,1)}, bf16[16,3072]{1,0:T(8,128)(2,1)S(1)}, u32[]{:S(2)}, u32[]{:S(2)}) collective-permute-start(bf16[16,3072]{1,0:T(8,128)(2,1)} %param.4), channel_id=1, source_target_pairs={{0,192},{64,0},{128,64},{192,128},{1,193},{65,1},{129,65},{193,129... | collective-permute-start | bytes 294920 | tf_op jit(solution)/shard_map/ppermute | solution.py:21
  8.1 3.2 %collective-permute-done = bf16[16,3072]{1,0:T(8,128)(2,1)S(1)} collective-permute-done((bf16[16,3072]{1,0:T(8,128)(2,1)}, bf16[16,3072]{1,0:T(8,128)(2,1)S(1)}, u32[]{:S(2)}, u32[]{:S(2)}) %collective-permute-start) | collective-permute-done | bytes 98336 | tf_op jit(solution)/shard_map/ppermute | solution.py:21
  12.3 1.3 %collective-permute-done.3 = bf16[64,3072]{1,0:T(8,128)(2,1)S(1)} collective-permute-done((bf16[64,3072]{1,0:T(8,128)(2,1)S(1)}, bf16[64,3072]{1,0:T(8,128)(2,1)S(1)}, u32[]{:S(2)}, u32[]{:S(2)}) %collective-permute-start.3) | collective-permute-done | bytes 393248 | tf_op jit(solution)/shard_map/ppermute | solution.py:21
  13.9 5.0 %collective-permute-start.12 = (bf16[128,1536]{1,0:T(8,128)(2,1)S(1)}, bf16[128,1536]{1,0:T(8,128)(2,1)S(1)}, u32[]{:S(2)}, u32[]{:S(2)}) collective-permute-start(bf16[128,1536]{1,0:T(8,128)(2,1)S(1)} %get-tuple-element.36), channel_id=1, source_target_pairs={{0,2},{1,15},{2,4},{3,1},{4,6},{5,3},{6,8},{7,5},{8,10},{9,7},{10,... | collective-permute-start | bytes 1179656 | tf_op jit(solution)/shard_map/ppermute | solution.py:31
  20.9 2.3 %collective-permute-start.9 = (bf16[128,768]{1,0:T(8,128)(2,1)}, bf16[128,768]{1,0:T(8,128)(2,1)}, u32[]{:S(2)}, u32[]{:S(2)}) collective-permute-start(bf16[128,768]{1,0:T(8,128)(2,1)} %get-tuple-element.34), channel_id=1, source_target_pairs={{0,192},{64,0},{128,64},{192,128},{1,193},{65,1},{129,65},{193,129... | collective-permute-start | bytes 589832 | tf_op jit(solution)/shard_map/ppermute | solution.py:21
  23.3 1.2 %collective-permute-start.8 = (bf16[128,768]{1,0:T(8,128)(2,1)}, bf16[128,768]{1,0:T(8,128)(2,1)}, u32[]{:S(2)}, u32[]{:S(2)}) collective-permute-start(bf16[128,768]{1,0:T(8,128)(2,1)} %get-tuple-element.35), channel_id=1, source_target_pairs={{0,128},{64,192},{128,0},{192,64},{1,129},{65,193},{129,1},{193,65... | collective-permute-start | bytes 589832 | tf_op jit(solution)/shard_map/ppermute | solution.py:21
  24.4 2.6 %collective-permute-start.14 = (bf16[128,1536]{1,0:T(8,128)(2,1)S(1)}, bf16[128,1536]{1,0:T(8,128)(2,1)S(1)}, u32[]{:S(2)}, u32[]{:S(2)}) collective-permute-start(bf16[128,1536]{1,0:T(8,128)(2,1)S(1)} %collective-permute-done.12), channel_id=1, source_target_pairs={{0,2},{1,15},{2,4},{3,1},{4,6},{5,3},{6,8},{7,5},{8,10},{9,7},{10,... | collective-permute-start | bytes 1179656 | tf_op jit(solution)/shard_map/ppermute | solution.py:31
  27.8 3.5 %collective-permute-start.5 = (bf16[128,1536]{1,0:T(8,128)(2,1)S(1)}, bf16[128,1536]{1,0:T(8,128)(2,1)}, u32[]{:S(2)}, u32[]{:S(2)}) collective-permute-start(bf16[128,1536]{1,0:T(8,128)(2,1)S(1)} %collective-permute-done.4), channel_id=1, source_target_pairs={{0,2},{1,15},{2,4},{3,1},{4,6},{5,3},{6,8},{7,5},{8,10},{9,7},{10,... | collective-permute-start | bytes 1179656 | tf_op jit(solution)/shard_map/ppermute | solution.py:31
  33.5 2.6 %collective-permute-start.10 = (bf16[3,128,768]{2,1,0:T(8,128)(2,1)S(1)}, bf16[3,128,768]{2,1,0:T(8,128)(2,1)S(1)}, u32[]{:S(2)}, u32[]{:S(2)}) collective-permute-start(bf16[3,128,768]{2,1,0:T(8,128)(2,1)S(1)} %pad_maximum_fusion.4.near), channel_id=1, source_target_pairs={{0,16},{1,49},{16,32},{17,1},{32,48},{33,17},{48,0},{49,33},{2,18}... | collective-permute-start | bytes 1769480 | tf_op jit(solution)/shard_map/ppermute | solution.py:31
  36.1 1.9 %collective-permute-start.16 = (bf16[128,1536]{1,0:T(8,128)(2,1)S(1)}, bf16[128,1536]{1,0:T(8,128)(2,1)S(1)}, u32[]{:S(2)}, u32[]{:S(2)}) collective-permute-start(bf16[128,1536]{1,0:T(8,128)(2,1)S(1)} %collective-permute-done.14), channel_id=1, source_target_pairs={{0,2},{1,15},{2,4},{3,1},{4,6},{5,3},{6,8},{7,5},{8,10},{9,7},{10,... | collective-permute-start | bytes 1179656 | tf_op jit(solution)/shard_map/ppermute | solution.py:31
  38.0 1.4 %collective-permute-start.6 = (bf16[128,1536]{1,0:T(8,128)(2,1)}, bf16[128,1536]{1,0:T(8,128)(2,1)S(1)}, u32[]{:S(2)}, u32[]{:S(2)}) collective-permute-start(bf16[128,1536]{1,0:T(8,128)(2,1)} %collective-permute-done.5), channel_id=1, source_target_pairs={{0,2},{1,15},{2,4},{3,1},{4,6},{5,3},{6,8},{7,5},{8,10},{9,7},{10,... | collective-permute-start | bytes 1179656 | tf_op jit(solution)/shard_map/ppermute | solution.py:31
  41.4 1.5 %collective-permute-done.10.far = bf16[3,128,768]{2,1,0:T(8,128)(2,1)S(1)} collective-permute-done((bf16[3,128,768]{2,1,0:T(8,128)(2,1)S(1)}, bf16[3,128,768]{2,1,0:T(8,128)(2,1)S(1)}, u32[]{:S(2)}, u32[]{:S(2)}) %collective-permute-start.10) | collective-permute-done | bytes 589856 | tf_op jit(solution)/shard_map/ppermute | solution.py:31
  42.9 4.6 %collective-permute-done.6 = bf16[128,1536]{1,0:T(8,128)(2,1)S(1)} collective-permute-done((bf16[128,1536]{1,0:T(8,128)(2,1)}, bf16[128,1536]{1,0:T(8,128)(2,1)S(1)}, u32[]{:S(2)}, u32[]{:S(2)}) %collective-permute-start.6) | collective-permute-done | bytes 393248 | tf_op jit(solution)/shard_map/ppermute | solution.py:31
  47.4 2.7 %collective-permute-start.11 = (bf16[128,1536]{1,0:T(8,128)(2,1)S(1)}, bf16[128,1536]{1,0:T(8,128)(2,1)S(1)}, u32[]{:S(2)}, u32[]{:S(2)}) collective-permute-start(bf16[128,1536]{1,0:T(8,128)(2,1)S(1)} %collective-permute-done.6), channel_id=1, source_target_pairs={{0,2},{1,15},{2,4},{3,1},{4,6},{5,3},{6,8},{7,5},{8,10},{9,7},{10,... | collective-permute-start | bytes 1179656 | tf_op jit(solution)/shard_map/ppermute | solution.py:31
  50.9 1.4 %fusion.2 = f32[1536,768]{1,0:T(8,128)S(1)} fusion(bf16[384,1536]{1,0:T(8,128)(2,1)S(1)} %pad_maximum_fusion.3, bf16[1024,768]{1,0:T(8,128)(2,1)S(1)} %shard_map.67), kind=kOutput, calls=%fused_computation.17 | convolution fusion | flops 905969664 | bytes 6488064 | tf_op jit(solution)/shard_map/dot_general | solution.py:187
  52.9 1.4 %fusion.4 = f32[1536,768]{1,0:T(8,128)S(1)} fusion(bf16[384,1536]{1,0:T(8,128)(2,1)S(1)} %pad_maximum_fusion.2, bf16[1024,768]{1,0:T(8,128)(2,1)S(1)} %shard_map.67), kind=kOutput, calls=%fused_computation.19 | convolution fusion | flops 905969664 | bytes 6488064 | tf_op jit(solution)/shard_map/dot_general | solution.py:187
  55.5 1.6 %convolution_add_fusion = f32[1536,768]{1,0:T(8,128)S(1)} fusion(f32[1536,768]{1,0:T(8,128)S(1)} %fusion.4, bf16[512,1536]{1,0:T(8,128)(2,1)S(1)} %pad_maximum_fusion, bf16[1024,768]{1,0:T(8,128)(2,1)S(1)} %shard_map.67), kind=kOutput, calls=%fused_computation.7 | convolution fusion | flops 1209139200 | bytes 11796480 | tf_op jit(solution)/shard_map/dot_general | solution.py:187
  59.7 1.7 %add_add_fusion.grad1 = f32[1536,768]{1,0:T(8,128)S(1)} fusion(f32[1536,768]{1,0:T(8,128)S(1)} %fusion.7, f32[1536,768]{1,0:T(8,128)S(1)} %fusion.2, bf16[512,1536]{1,0:T(8,128)(2,1)S(1)} %pad_maximum_fusion.1, bf16[1024,768]{1,0:T(8,128)(2,1)S(1)} %shard_map.67), kind=kOutput, calls=%fused_computation.2 | convolution fusion | flops 1210318848 | bytes 16515072 | tf_op jit(solution)/shard_map/dot_general | solution.py:187
  62.6 1.8 %collective-permute-start.24 = (f32[768]{0:T(1024)S(1)}, f32[768]{0:T(1024)S(1)}, u32[]{:S(2)}, u32[]{:S(2)}) collective-permute-start(f32[768]{0:T(1024)S(1)} %add.104), channel_id=1, source_target_pairs={{0,48},{16,0},{32,16},{48,32},{1,49},{17,1},{33,17},{49,33},{2,50}... | collective-permute-start | bytes 9224 | tf_op jit(solution)/shard_map/ppermute | solution.py:21
  64.3 1.7 %collective-permute-start.22 = (f32[768]{0:T(1024)S(1)}, f32[768]{0:T(1024)S(1)}, u32[]{:S(2)}, u32[]{:S(2)}) collective-permute-start(f32[768]{0:T(1024)S(1)} %add.104), channel_id=1, source_target_pairs={{0,32},{16,48},{32,0},{48,16},{1,33},{17,49},{33,1},{49,17},{2,34}... | collective-permute-start | bytes 9224 | tf_op jit(solution)/shard_map/ppermute | solution.py:21
  66.0 1.9 %collective-permute-done.23 = f32[768]{0:T(1024)S(1)} collective-permute-done((f32[768]{0:T(1024)S(1)}, f32[768]{0:T(1024)S(1)}, u32[]{:S(2)}, u32[]{:S(2)}) %collective-permute-start.23) | collective-permute-done | bytes 3104 | tf_op jit(solution)/shard_map/ppermute | solution.py:21
  69.9 1.9 %collective-permute-start.25 = (f32[48,128]{1,0:T(8,128)S(1)}, f32[48,128]{1,0:T(8,128)S(1)}, u32[]{:S(2)}, u32[]{:S(2)}) collective-permute-start(f32[48,128]{1,0:T(8,128)S(1)} %pad_maximum_fusion.6), channel_id=1, source_target_pairs={{0,1},{1,0},{2,3},{3,2},{4,5},{5,4},{6,7},{7,6},{8,9},{9,8},{10,11... | collective-permute-start | bytes 73736 | tf_op jit(solution)/shard_map/ppermute | solution.py:21
  72.7 3.0 %collective-permute-start.27 = (f32[48,128]{1,0:T(8,128)S(1)}, f32[48,128]{1,0:T(8,128)S(1)}, u32[]{:S(2)}, u32[]{:S(2)}) collective-permute-start(f32[48,128]{1,0:T(8,128)S(1)} %fusion.22), channel_id=1, source_target_pairs={{0,64},{1,193},{64,128},{65,1},{128,192},{129,65},{192,0},{193,129... | collective-permute-start | bytes 73736 | tf_op jit(solution)/shard_map/ppermute | solution.py:31
  76.6 1.5 %collective-permute-start.28 = (f32[48,128]{1,0:T(8,128)S(1)}, f32[48,128]{1,0:T(8,128)S(1)}, u32[]{:S(2)}, u32[]{:S(2)}) collective-permute-start(f32[48,128]{1,0:T(8,128)S(1)} %collective-permute-done.27), channel_id=1, source_target_pairs={{0,1},{1,0},{2,3},{3,2},{4,5},{5,4},{6,7},{7,6},{8,9},{9,8},{10,11... | collective-permute-start | bytes 73736 | tf_op jit(solution)/shard_map/ppermute | solution.py:21
  78.1 1.7 %collective-permute-done.26 = f32[48,128]{1,0:T(8,128)S(1)} collective-permute-done((f32[48,128]{1,0:T(8,128)S(1)}, f32[48,128]{1,0:T(8,128)S(1)}, u32[]{:S(2)}, u32[]{:S(2)}) %collective-permute-start.26) | collective-permute-done | bytes 24608 | tf_op jit(solution)/shard_map/ppermute | solution.py:21
  79.9 2.7 %collective-permute-done.29 = f32[48,128]{1,0:T(8,128)S(1)} collective-permute-done((f32[48,128]{1,0:T(8,128)S(1)}, f32[48,128]{1,0:T(8,128)S(1)}, u32[]{:S(2)}, u32[]{:S(2)}) %collective-permute-start.29) | collective-permute-done | bytes 24608 | tf_op jit(solution)/shard_map/ppermute | solution.py:39
  83.3 4.7 %collective-permute-start.30 = (f32[48,128]{1,0:T(8,128)S(1)}, f32[48,128]{1,0:T(8,128)S(1)}, u32[]{:S(2)}, u32[]{:S(2)}) collective-permute-start(f32[48,128]{1,0:T(8,128)S(1)} %add.113.p0), channel_id=1, source_target_pairs={{0,8},{2,10},{4,12},{6,14},{8,0},{10,2},{12,4},{14,6},{1,9},{3,11}... | collective-permute-start | bytes 73736 | tf_op jit(solution)/shard_map/ppermute | solution.py:21
  88.0 1.9 %collective-permute-start.32 = (f32[48,128]{1,0:T(8,128)S(1)}, f32[48,128]{1,0:T(8,128)S(1)}, u32[]{:S(2)}, u32[]{:S(2)}) collective-permute-start(f32[48,128]{1,0:T(8,128)S(1)} %collective-permute-done.31.p2), channel_id=1, source_target_pairs={{0,1},{1,0},{2,3},{3,2},{4,5},{5,4},{6,7},{7,6},{8,9},{9,8},{10,11... | collective-permute-start | bytes 73736 | tf_op jit(solution)/shard_map/ppermute | solution.py:21
  91.4 2.7 %collective-permute-start.34 = (f32[2,128]{1,0:T(2,128)S(1)}, f32[2,128]{1,0:T(2,128)S(1)}, u32[]{:S(2)}, u32[]{:S(2)}) collective-permute-start(f32[2,128]{1,0:T(2,128)S(1)} %get-tuple-element.22.p0), channel_id=1, source_target_pairs={{0,16},{1,49},{16,32},{17,1},{32,48},{33,17},{48,0},{49,33},{2,18}... | collective-permute-start | bytes 3080 | tf_op jit(solution)/shard_map/ppermute | solution.py:31
  94.8 3.9 %collective-permute-start.35 = (f32[2,128]{1,0:T(2,128)S(1)}, f32[2,128]{1,0:T(2,128)S(1)}, u32[]{:S(2)}, u32[]{:S(2)}) collective-permute-start(f32[2,128]{1,0:T(2,128)S(1)} %collective-permute-done.34.p2), channel_id=1, source_target_pairs={{0,1},{1,0},{2,3},{3,2},{4,5},{5,4},{6,7},{7,6},{8,9},{9,8},{10,11... | collective-permute-start | bytes 3080 | tf_op jit(solution)/shard_map/ppermute | solution.py:21
  99.5 3.9 %shard_map.69 = f32[3072,768]{1,0:T(8,128)} custom-call(s32[1]{0:T(128)} %bitcast.core, f32[2,128]{1,0:T(2,128)S(1)} %get-tuple-element.22.p0, f32[2,128]{1,0:T(2,128)S(1)} %collective-permute-done.33.p1, f32[2,128]{1,0:T(2,128)S(1)} %collective-permute-done.34.p2, f32[2,128]{1,0:T(2,128)S(1)} %collective-permute-done.35.p3, ...), custom_call_target="tpu_custom_call" | custom-call | tf_op jit(solution)/shard_map/pallas_call | solution.py:142
  (80 shorter events, 23.3 us)
Async XLA Ops:
  0.6 10.7 %collective-permute-start.1 = (bf16[16,3072]{1,0:T(8,128)(2,1)}, bf16[16,3072]{1,0:T(8,128)(2,1)S(1)}, u32[]{:S(2)}, u32[]{:S(2)}) collective-permute-start(bf16[16,3072]{1,0:T(8,128)(2,1)} %param.4), channel_id=1, source_target_pairs={{0,128},{64,192},{128,0},{192,64},{1,129},{65,193},{129,1},{193,65... | collective-permute-start | bytes 294920 | tf_op jit(solution)/shard_map/ppermute | solution.py:21
  4.5 6.9 %collective-permute-start = (bf16[16,3072]{1,0:T(8,128)(2,1)}, bf16[16,3072]{1,0:T(8,128)(2,1)S(1)}, u32[]{:S(2)}, u32[]{:S(2)}) collective-permute-start(bf16[16,3072]{1,0:T(8,128)(2,1)} %param.4), channel_id=1, source_target_pairs={{0,64},{64,128},{128,192},{192,0},{1,65},{65,129},{129,193},{193,1... | collective-permute-start | bytes 294920 | tf_op jit(solution)/shard_map/ppermute | solution.py:21
  4.9 6.5 %collective-permute-start.2 = (bf16[16,3072]{1,0:T(8,128)(2,1)}, bf16[16,3072]{1,0:T(8,128)(2,1)S(1)}, u32[]{:S(2)}, u32[]{:S(2)}) collective-permute-start(bf16[16,3072]{1,0:T(8,128)(2,1)} %param.4), channel_id=1, source_target_pairs={{0,192},{64,0},{128,64},{192,128},{1,193},{65,1},{129,65},{193,129... | collective-permute-start | bytes 294920 | tf_op jit(solution)/shard_map/ppermute | solution.py:21
  13.9 10.6 %collective-permute-start.12 = (bf16[128,1536]{1,0:T(8,128)(2,1)S(1)}, bf16[128,1536]{1,0:T(8,128)(2,1)S(1)}, u32[]{:S(2)}, u32[]{:S(2)}) collective-permute-start(bf16[128,1536]{1,0:T(8,128)(2,1)S(1)} %get-tuple-element.36), channel_id=1, source_target_pairs={{0,2},{1,15},{2,4},{3,1},{4,6},{5,3},{6,8},{7,5},{8,10},{9,7},{10,... | collective-permute-start | bytes 1179656 | tf_op jit(solution)/shard_map/ppermute | solution.py:31
  18.8 8.9 %collective-permute-start.4 = (bf16[128,1536]{1,0:T(8,128)(2,1)S(1)}, bf16[128,1536]{1,0:T(8,128)(2,1)S(1)}, u32[]{:S(2)}, u32[]{:S(2)}) collective-permute-start(bf16[128,1536]{1,0:T(8,128)(2,1)S(1)} %get-tuple-element.37), channel_id=1, source_target_pairs={{0,2},{1,15},{2,4},{3,1},{4,6},{5,3},{6,8},{7,5},{8,10},{9,7},{10,... | collective-permute-start | bytes 1179656 | tf_op jit(solution)/shard_map/ppermute | solution.py:31
  20.4 10.9 %collective-permute-start.7 = (bf16[128,768]{1,0:T(8,128)(2,1)S(1)}, bf16[128,768]{1,0:T(8,128)(2,1)}, u32[]{:S(2)}, u32[]{:S(2)}) collective-permute-start(bf16[128,768]{1,0:T(8,128)(2,1)S(1)} %get-tuple-element.33), channel_id=1, source_target_pairs={{0,64},{64,128},{128,192},{192,0},{1,65},{65,129},{129,193},{193,1... | collective-permute-start | bytes 589832 | tf_op jit(solution)/shard_map/ppermute | solution.py:21
  20.9 10.4 %collective-permute-start.9 = (bf16[128,768]{1,0:T(8,128)(2,1)}, bf16[128,768]{1,0:T(8,128)(2,1)}, u32[]{:S(2)}, u32[]{:S(2)}) collective-permute-start(bf16[128,768]{1,0:T(8,128)(2,1)} %get-tuple-element.34), channel_id=1, source_target_pairs={{0,192},{64,0},{128,64},{192,128},{1,193},{65,1},{129,65},{193,129... | collective-permute-start | bytes 589832 | tf_op jit(solution)/shard_map/ppermute | solution.py:21
  23.3 9.0 %collective-permute-start.8 = (bf16[128,768]{1,0:T(8,128)(2,1)}, bf16[128,768]{1,0:T(8,128)(2,1)}, u32[]{:S(2)}, u32[]{:S(2)}) collective-permute-start(bf16[128,768]{1,0:T(8,128)(2,1)} %get-tuple-element.35), channel_id=1, source_target_pairs={{0,128},{64,192},{128,0},{192,64},{1,129},{65,193},{129,1},{193,65... | collective-permute-start | bytes 589832 | tf_op jit(solution)/shard_map/ppermute | solution.py:21
  24.4 11.7 %collective-permute-start.14 = (bf16[128,1536]{1,0:T(8,128)(2,1)S(1)}, bf16[128,1536]{1,0:T(8,128)(2,1)S(1)}, u32[]{:S(2)}, u32[]{:S(2)}) collective-permute-start(bf16[128,1536]{1,0:T(8,128)(2,1)S(1)} %collective-permute-done.12), channel_id=1, source_target_pairs={{0,2},{1,15},{2,4},{3,1},{4,6},{5,3},{6,8},{7,5},{8,10},{9,7},{10,... | collective-permute-start | bytes 1179656 | tf_op jit(solution)/shard_map/ppermute | solution.py:31
  27.8 10.3 %collective-permute-start.5 = (bf16[128,1536]{1,0:T(8,128)(2,1)S(1)}, bf16[128,1536]{1,0:T(8,128)(2,1)}, u32[]{:S(2)}, u32[]{:S(2)}) collective-permute-start(bf16[128,1536]{1,0:T(8,128)(2,1)S(1)} %collective-permute-done.4), channel_id=1, source_target_pairs={{0,2},{1,15},{2,4},{3,1},{4,6},{5,3},{6,8},{7,5},{8,10},{9,7},{10,... | collective-permute-start | bytes 1179656 | tf_op jit(solution)/shard_map/ppermute | solution.py:31
  31.3 8.1 %collective-permute-start.13 = (bf16[128,1536]{1,0:T(8,128)(2,1)S(1)}, bf16[128,1536]{1,0:T(8,128)(2,1)}, u32[]{:S(2)}, u32[]{:S(2)}) collective-permute-start(bf16[128,1536]{1,0:T(8,128)(2,1)S(1)} %collective-permute-done.12), channel_id=1, source_target_pairs={{0,1},{1,0},{2,3},{3,2},{4,5},{5,4},{6,7},{7,6},{8,9},{9,8},{10,11... | collective-permute-start | bytes 1179656 | tf_op jit(solution)/shard_map/ppermute | solution.py:21
  31.3 9.2 %collective-permute-start.18 = (bf16[128,1536]{1,0:T(8,128)(2,1)S(1)}, bf16[128,1536]{1,0:T(8,128)(2,1)S(1)}, u32[]{:S(2)}, u32[]{:S(2)}) collective-permute-start(bf16[128,1536]{1,0:T(8,128)(2,1)S(1)} %collective-permute-done.4), channel_id=1, source_target_pairs={{0,1},{1,0},{2,3},{3,2},{4,5},{5,4},{6,7},{7,6},{8,9},{9,8},{10,11... | collective-permute-start | bytes 1179656 | tf_op jit(solution)/shard_map/ppermute | solution.py:21
  33.5 9.4 %collective-permute-start.10 = (bf16[3,128,768]{2,1,0:T(8,128)(2,1)S(1)}, bf16[3,128,768]{2,1,0:T(8,128)(2,1)S(1)}, u32[]{:S(2)}, u32[]{:S(2)}) collective-permute-start(bf16[3,128,768]{2,1,0:T(8,128)(2,1)S(1)} %pad_maximum_fusion.4.near), channel_id=1, source_target_pairs={{0,16},{1,49},{16,32},{17,1},{32,48},{33,17},{48,0},{49,33},{2,18}... | collective-permute-start | bytes 1769480 | tf_op jit(solution)/shard_map/ppermute | solution.py:31
  36.1 14.7 %collective-permute-start.16 = (bf16[128,1536]{1,0:T(8,128)(2,1)S(1)}, bf16[128,1536]{1,0:T(8,128)(2,1)S(1)}, u32[]{:S(2)}, u32[]{:S(2)}) collective-permute-start(bf16[128,1536]{1,0:T(8,128)(2,1)S(1)} %collective-permute-done.14), channel_id=1, source_target_pairs={{0,2},{1,15},{2,4},{3,1},{4,6},{5,3},{6,8},{7,5},{8,10},{9,7},{10,... | collective-permute-start | bytes 1179656 | tf_op jit(solution)/shard_map/ppermute | solution.py:31
  38.0 9.4 %collective-permute-start.6 = (bf16[128,1536]{1,0:T(8,128)(2,1)}, bf16[128,1536]{1,0:T(8,128)(2,1)S(1)}, u32[]{:S(2)}, u32[]{:S(2)}) collective-permute-start(bf16[128,1536]{1,0:T(8,128)(2,1)} %collective-permute-done.5), channel_id=1, source_target_pairs={{0,2},{1,15},{2,4},{3,1},{4,6},{5,3},{6,8},{7,5},{8,10},{9,7},{10,... | collective-permute-start | bytes 1179656 | tf_op jit(solution)/shard_map/ppermute | solution.py:31
  40.6 13.8 %collective-permute-start.15 = (bf16[128,1536]{1,0:T(8,128)(2,1)S(1)}, bf16[128,1536]{1,0:T(8,128)(2,1)S(1)}, u32[]{:S(2)}, u32[]{:S(2)}) collective-permute-start(bf16[128,1536]{1,0:T(8,128)(2,1)S(1)} %collective-permute-done.14), channel_id=1, source_target_pairs={{0,1},{1,0},{2,3},{3,2},{4,5},{5,4},{6,7},{7,6},{8,9},{9,8},{10,11... | collective-permute-start | bytes 1179656 | tf_op jit(solution)/shard_map/ppermute | solution.py:21
  40.9 16.3 %collective-permute-start.19 = (bf16[128,1536]{1,0:T(8,128)(2,1)}, bf16[128,1536]{1,0:T(8,128)(2,1)S(1)}, u32[]{:S(2)}, u32[]{:S(2)}) collective-permute-start(bf16[128,1536]{1,0:T(8,128)(2,1)} %collective-permute-done.5), channel_id=1, source_target_pairs={{0,1},{1,0},{2,3},{3,2},{4,5},{5,4},{6,7},{7,6},{8,9},{9,8},{10,11... | collective-permute-start | bytes 1179656 | tf_op jit(solution)/shard_map/ppermute | solution.py:21
  47.4 9.6 %collective-permute-start.11 = (bf16[128,1536]{1,0:T(8,128)(2,1)S(1)}, bf16[128,1536]{1,0:T(8,128)(2,1)S(1)}, u32[]{:S(2)}, u32[]{:S(2)}) collective-permute-start(bf16[128,1536]{1,0:T(8,128)(2,1)S(1)} %collective-permute-done.6), channel_id=1, source_target_pairs={{0,2},{1,15},{2,4},{3,1},{4,6},{5,3},{6,8},{7,5},{8,10},{9,7},{10,... | collective-permute-start | bytes 1179656 | tf_op jit(solution)/shard_map/ppermute | solution.py:31
  50.8 3.6 %collective-permute-start.17 = (bf16[128,1536]{1,0:T(8,128)(2,1)S(1)}, bf16[128,1536]{1,0:T(8,128)(2,1)S(1)}, u32[]{:S(2)}, u32[]{:S(2)}) collective-permute-start(bf16[128,1536]{1,0:T(8,128)(2,1)S(1)} %collective-permute-done.16), channel_id=1, source_target_pairs={{0,1},{1,0},{2,3},{3,2},{4,5},{5,4},{6,7},{7,6},{8,9},{9,8},{10,11... | collective-permute-start | bytes 1179656 | tf_op jit(solution)/shard_map/ppermute | solution.py:21
  52.3 4.8 %collective-permute-start.20 = (bf16[128,1536]{1,0:T(8,128)(2,1)S(1)}, bf16[128,1536]{1,0:T(8,128)(2,1)S(1)}, u32[]{:S(2)}, u32[]{:S(2)}) collective-permute-start(bf16[128,1536]{1,0:T(8,128)(2,1)S(1)} %collective-permute-done.6), channel_id=1, source_target_pairs={{0,1},{1,0},{2,3},{3,2},{4,5},{5,4},{6,7},{7,6},{8,9},{9,8},{10,11... | collective-permute-start | bytes 1179656 | tf_op jit(solution)/shard_map/ppermute | solution.py:21
  62.6 3.5 %collective-permute-start.24 = (f32[768]{0:T(1024)S(1)}, f32[768]{0:T(1024)S(1)}, u32[]{:S(2)}, u32[]{:S(2)}) collective-permute-start(f32[768]{0:T(1024)S(1)} %add.104), channel_id=1, source_target_pairs={{0,48},{16,0},{32,16},{48,32},{1,49},{17,1},{33,17},{49,33},{2,50}... | collective-permute-start | bytes 9224 | tf_op jit(solution)/shard_map/ppermute | solution.py:21
  64.3 3.7 %collective-permute-start.23 = (f32[768]{0:T(1024)S(1)}, f32[768]{0:T(1024)S(1)}, u32[]{:S(2)}, u32[]{:S(2)}) collective-permute-start(f32[768]{0:T(1024)S(1)} %add.104), channel_id=1, source_target_pairs={{0,16},{16,32},{32,48},{48,0},{1,17},{17,33},{33,49},{49,1},{2,18}... | collective-permute-start | bytes 9224 | tf_op jit(solution)/shard_map/ppermute | solution.py:21
  64.3 4.0 %collective-permute-start.22 = (f32[768]{0:T(1024)S(1)}, f32[768]{0:T(1024)S(1)}, u32[]{:S(2)}, u32[]{:S(2)}) collective-permute-start(f32[768]{0:T(1024)S(1)} %add.104), channel_id=1, source_target_pairs={{0,32},{16,48},{32,0},{48,16},{1,33},{17,49},{33,1},{49,17},{2,34}... | collective-permute-start | bytes 9224 | tf_op jit(solution)/shard_map/ppermute | solution.py:21
  72.7 3.9 %collective-permute-start.27 = (f32[48,128]{1,0:T(8,128)S(1)}, f32[48,128]{1,0:T(8,128)S(1)}, u32[]{:S(2)}, u32[]{:S(2)}) collective-permute-start(f32[48,128]{1,0:T(8,128)S(1)} %fusion.22), channel_id=1, source_target_pairs={{0,64},{1,193},{64,128},{65,1},{128,192},{129,65},{192,0},{193,129... | collective-permute-start | bytes 73736 | tf_op jit(solution)/shard_map/ppermute | solution.py:31
  75.6 4.2 %collective-permute-start.26 = (f32[48,128]{1,0:T(8,128)S(1)}, f32[48,128]{1,0:T(8,128)S(1)}, u32[]{:S(2)}, u32[]{:S(2)}) collective-permute-start(f32[48,128]{1,0:T(8,128)S(1)} %fusion.22), channel_id=1, source_target_pairs={{0,128},{64,192},{128,0},{192,64},{1,129},{65,193},{129,1},{193,65... | collective-permute-start | bytes 73736 | tf_op jit(solution)/shard_map/ppermute | solution.py:21
  76.6 3.2 %collective-permute-start.28 = (f32[48,128]{1,0:T(8,128)S(1)}, f32[48,128]{1,0:T(8,128)S(1)}, u32[]{:S(2)}, u32[]{:S(2)}) collective-permute-start(f32[48,128]{1,0:T(8,128)S(1)} %collective-permute-done.27), channel_id=1, source_target_pairs={{0,1},{1,0},{2,3},{3,2},{4,5},{5,4},{6,7},{7,6},{8,9},{9,8},{10,11... | collective-permute-start | bytes 73736 | tf_op jit(solution)/shard_map/ppermute | solution.py:21
  79.8 2.8 %collective-permute-start.29 = (f32[48,128]{1,0:T(8,128)S(1)}, f32[48,128]{1,0:T(8,128)S(1)}, u32[]{:S(2)}, u32[]{:S(2)}) collective-permute-start(f32[48,128]{1,0:T(8,128)S(1)} %add_add_fusion.1), channel_id=1, source_target_pairs={{0,2},{2,0},{4,6},{6,4},{8,10},{10,8},{12,14},{14,12},{1,3},{3,1},... | collective-permute-start | bytes 73736 | tf_op jit(solution)/shard_map/ppermute | solution.py:39
  82.6 5.4 %collective-permute-start.31 = (f32[48,128]{1,0:T(8,128)S(1)}, f32[48,128]{1,0:T(8,128)S(1)}, u32[]{:S(2)}, u32[]{:S(2)}) collective-permute-start(f32[48,128]{1,0:T(8,128)S(1)} %add.113.p0), channel_id=1, source_target_pairs={{0,4},{1,13},{2,6},{3,15},{4,8},{5,1},{6,10},{7,3},{8,12},{9,5},{1... | collective-permute-start | bytes 73736 | tf_op jit(solution)/shard_map/ppermute | solution.py:31
  83.3 6.6 %collective-permute-start.30 = (f32[48,128]{1,0:T(8,128)S(1)}, f32[48,128]{1,0:T(8,128)S(1)}, u32[]{:S(2)}, u32[]{:S(2)}) collective-permute-start(f32[48,128]{1,0:T(8,128)S(1)} %add.113.p0), channel_id=1, source_target_pairs={{0,8},{2,10},{4,12},{6,14},{8,0},{10,2},{12,4},{14,6},{1,9},{3,11}... | collective-permute-start | bytes 73736 | tf_op jit(solution)/shard_map/ppermute | solution.py:21
  91.4 3.4 %collective-permute-start.34 = (f32[2,128]{1,0:T(2,128)S(1)}, f32[2,128]{1,0:T(2,128)S(1)}, u32[]{:S(2)}, u32[]{:S(2)}) collective-permute-start(f32[2,128]{1,0:T(2,128)S(1)} %get-tuple-element.22.p0), channel_id=1, source_target_pairs={{0,16},{1,49},{16,32},{17,1},{32,48},{33,17},{48,0},{49,33},{2,18}... | collective-permute-start | bytes 3080 | tf_op jit(solution)/shard_map/ppermute | solution.py:31
  94.1 4.6 %collective-permute-start.33 = (f32[2,128]{1,0:T(2,128)S(1)}, f32[2,128]{1,0:T(2,128)S(1)}, u32[]{:S(2)}, u32[]{:S(2)}) collective-permute-start(f32[2,128]{1,0:T(2,128)S(1)} %get-tuple-element.22.p0), channel_id=1, source_target_pairs={{0,32},{16,48},{32,0},{48,16},{1,33},{17,49},{33,1},{49,17},{2,34}... | collective-permute-start | bytes 3080 | tf_op jit(solution)/shard_map/ppermute | solution.py:21
  94.8 4.7 %collective-permute-start.35 = (f32[2,128]{1,0:T(2,128)S(1)}, f32[2,128]{1,0:T(2,128)S(1)}, u32[]{:S(2)}, u32[]{:S(2)}) collective-permute-start(f32[2,128]{1,0:T(2,128)S(1)} %collective-permute-done.34.p2), channel_id=1, source_target_pairs={{0,1},{1,0},{2,3},{3,2},{4,5},{5,4},{6,7},{7,6},{8,9},{9,8},{10,11... | collective-permute-start | bytes 3080 | tf_op jit(solution)/shard_map/ppermute | solution.py:21
  (7 other events, 57.2 us)

commit v4 on v3

--- a/solution.py
+++ b/solution.py
@@ -10,7 +10,6 @@
 DECAY = 0.7
 CLIP = 1.0
 SIZE = {"dp": 4, "row": 4, "z": 8, "core": 2}
-GROUPS = ((0, 3), (3, 5), (5, 7), (7, 8))
 
 
 SMALL = pltpu.CompilerParams(vmem_limit_bytes=6 * 2**20)
@@ -181,9 +180,7 @@
         halves[1] += [here[1], swap(here[0])]
         return here
 
-    def product(h, lo, hi):
-        (tokens,) = tie(jnp.concatenate(halves[h][lo:hi], axis=0))
-        rows = b[lo * 128 : hi * 128]
+    def product(tokens, rows):
         return lax.dot_general(
             tokens, rows, (((0,), (0,)), ((), ())), preferred_element_type=jnp.float32
         )
@@ -192,12 +189,16 @@
     here[0], parcels = tie(here[0], parcels)
     far = apart(here[0], "z")
     b = order(jnp.stack([z, core, row % 2]), *parcels)
-    grads = [product(h, 0, 3) for h in (0, 1)]
-    grads = [grads[h] + product(h, 3, 7) for h in (0, 1)]
-    far, grads[0] = tie(far, grads[0])
-    halves[0].append(far)
-    halves[1].append(swap(far))
-    (grads,) = tie([grads[h] + product(h, 7, 8) for h in (0, 1)])
+    blank = jnp.zeros((128, 1536), jnp.bfloat16)
+    early, late = (
+        [jnp.concatenate((half + [blank])[i : i + 4], axis=0) for half in halves] for i in (0, 4)
+    )
+    (early,) = tie(early)
+    grads = [product(x, b[:512]) for x in early]
+    far, grads, late = tie(far, grads, late)
+    for h, x in enumerate((far, swap(far))):
+        (tokens,) = tie(lax.dynamic_update_slice(late[h], x, (384, 0)))
+        (grads[h],) = tie(grads[h] + product(tokens, b[512:]))
 
     col_part = sum(jnp.sum(grad * grad, axis=0) for grad in grads)
     col_sum = total(col_part, "row", 1)

time: 104 us -> 99.4 us (0.956)
  waiting for transfers between devices: 23.1 us -> 18.9 us
  other arithmetic: 6.63 us -> 8.57 us
  matrix products: 7.68 us -> 5.77 us
    ppermute x11, waiting for transfers between devices: 8.24 us -> 3.83 us  [apart(): return lax.ppermute(x, (axis, 'core'), pairs)]
    dot_general x6 -> x4, matrix products: 7.68 us -> 5.77 us  [product(): lax.dot_general(tokens, rows, (((0,), (0,)), ((), ())), preferred_element...]
    concatenate x4 -> x3, other arithmetic: 2.36 us -> 3.7 us  [on_device(): jnp.concatenate((half + [blank])[i:i + 4], axis=0)]
    ppermute x11, starting transfers between devices: 26.8 us -> 25.4 us  [apart(): return lax.ppermute(x, (axis, 'core'), pairs)]
  transfers between devices with their start and end apart: 36 -> 36, of which waited for: 16 -> 18; matrix products, arithmetic and copies ran while one was open for 10% -> 11% of each run, Pallas kernels for 1% -> 1%
where the time goes in v4:
time: 99.4 us; the launch traced here: 99.2 us
  starting transfers between devices  57.8 us (58%)
  waiting for transfers between devices  18.9 us (19%)
  other arithmetic  8.57 us (9%)
  matrix products  5.77 us (6%)
  Pallas kernels  5.19 us (5%)
  local copies, waits for them, and re-layouts  1.91 us (2%)
  between operations  1.08 us (1%)
    ppermute x24, starting transfers between devices, shift(): return lax.ppermute(x, axis, [(i, (i + step) % n) for i in range(n)])  32.2 us
    ppermute x11, starting transfers between devices, apart(): return lax.ppermute(x, (axis, 'core'), pairs)  25.4 us
    ppermute x24, waiting for transfers between devices, shift(): return lax.ppermute(x, axis, [(i, (i + step) % n) for i in range(n)])  12.4 us
    dot_general x4, matrix products, product(): lax.dot_general(tokens, rows, (((0,), (0,)), ((), ())), preferred_element...  5.77 us
    pallas_call x1, Pallas kernels, update_call(): pl.pallas_call(update_kernel, out_shape=jax.ShapeDtypeStruct((3072, 768),...  3.88 us
    ppermute x11, waiting for transfers between devices, apart(): return lax.ppermute(x, (axis, 'core'), pairs)  3.83 us
    concatenate x3, other arithmetic, on_device(): jnp.concatenate((half + [blank])[i:i + 4], axis=0)  3.7 us
    ppermute x1, waiting for transfers between devices, flip(): return lax.ppermute(x, axis, [(i, i ^ 1) for i in range(SIZE[axis])])  2.66 us
  transfers between devices with their start and end apart: 36, of which 18 were waited for; matrix products, arithmetic and copies ran while one was open for 11% of the time, Pallas kernels for 1%

profile of v4, /device:TPU:1, one launch (start us, length us, event | category | flops | bytes accessed | tf_op | source)
XLA Modules:
  0.0 99.2 jit_solution(13656029160035654314)
XLA Ops:
  0.6 3.8 %collective-permute-start.1 = (bf16[16,3072]{1,0:T(8,128)(2,1)}, bf16[16,3072]{1,0:T(8,128)(2,1)S(1)}, u32[]{:S(2)}, u32[]{:S(2)}) collective-permute-start(bf16[16,3072]{1,0:T(8,128)(2,1)} %param.4), channel_id=1, source_target_pairs={{0,128},{64,192},{128,0},{192,64},{1,129},{65,193},{129,1},{193,65... | collective-permute-start | bytes 294920 | tf_op jit(solution)/shard_map/ppermute | solution.py:20
  4.9 2.3 %collective-permute-start.2 = (bf16[16,3072]{1,0:T(8,128)(2,1)}, bf16[16,3072]{1,0:T(8,128)(2,1)S(1)}, u32[]{:S(2)}, u32[]{:S(2)}) collective-permute-start(bf16[16,3072]{1,0:T(8,128)(2,1)} %param.4), channel_id=1, source_target_pairs={{0,192},{64,0},{128,64},{192,128},{1,193},{65,1},{129,65},{193,129... | collective-permute-start | bytes 294920 | tf_op jit(solution)/shard_map/ppermute | solution.py:20
  8.1 3.2 %collective-permute-done = bf16[16,3072]{1,0:T(8,128)(2,1)S(1)} collective-permute-done((bf16[16,3072]{1,0:T(8,128)(2,1)}, bf16[16,3072]{1,0:T(8,128)(2,1)S(1)}, u32[]{:S(2)}, u32[]{:S(2)}) %collective-permute-start) | collective-permute-done | bytes 98336 | tf_op jit(solution)/shard_map/ppermute | solution.py:20
  12.3 1.3 %collective-permute-done.3 = bf16[64,3072]{1,0:T(8,128)(2,1)S(1)} collective-permute-done((bf16[64,3072]{1,0:T(8,128)(2,1)S(1)}, bf16[64,3072]{1,0:T(8,128)(2,1)S(1)}, u32[]{:S(2)}, u32[]{:S(2)}) %collective-permute-start.3) | collective-permute-done | bytes 393248 | tf_op jit(solution)/shard_map/ppermute | solution.py:20
  13.8 5.0 %collective-permute-start.4 = (bf16[128,1536]{1,0:T(8,128)(2,1)S(1)}, bf16[128,1536]{1,0:T(8,128)(2,1)S(1)}, u32[]{:S(2)}, u32[]{:S(2)}) collective-permute-start(bf16[128,1536]{1,0:T(8,128)(2,1)S(1)} %get-tuple-element.43), channel_id=1, source_target_pairs={{0,2},{1,15},{2,4},{3,1},{4,6},{5,3},{6,8},{7,5},{8,10},{9,7},{10,... | collective-permute-start | bytes 1179656 | tf_op jit(solution)/shard_map/ppermute | solution.py:30
  21.0 2.3 %collective-permute-start.9 = (bf16[128,768]{1,0:T(8,128)(2,1)}, bf16[128,768]{1,0:T(8,128)(2,1)}, u32[]{:S(2)}, u32[]{:S(2)}) collective-permute-start(bf16[128,768]{1,0:T(8,128)(2,1)} %get-tuple-element.40), channel_id=1, source_target_pairs={{0,192},{64,0},{128,64},{192,128},{1,193},{65,1},{129,65},{193,129... | collective-permute-start | bytes 589832 | tf_op jit(solution)/shard_map/ppermute | solution.py:20
  24.5 2.6 %collective-permute-start.5 = (bf16[128,1536]{1,0:T(8,128)(2,1)S(1)}, bf16[128,1536]{1,0:T(8,128)(2,1)S(1)}, u32[]{:S(2)}, u32[]{:S(2)}) collective-permute-start(bf16[128,1536]{1,0:T(8,128)(2,1)S(1)} %collective-permute-done.4), channel_id=1, source_target_pairs={{0,2},{1,15},{2,4},{3,1},{4,6},{5,3},{6,8},{7,5},{8,10},{9,7},{10,... | collective-permute-start | bytes 1179656 | tf_op jit(solution)/shard_map/ppermute | solution.py:30
  27.7 1.7 %collective-permute-start.13 = (bf16[128,1536]{1,0:T(8,128)(2,1)S(1)}, bf16[128,1536]{1,0:T(8,128)(2,1)}, u32[]{:S(2)}, u32[]{:S(2)}) collective-permute-start(bf16[128,1536]{1,0:T(8,128)(2,1)S(1)} %collective-permute-done.12), channel_id=1, source_target_pairs={{0,1},{1,0},{2,3},{3,2},{4,5},{5,4},{6,7},{7,6},{8,9},{9,8},{10,11... | collective-permute-start | bytes 1179656 | tf_op jit(solution)/shard_map/ppermute | solution.py:20
  29.5 1.9 %collective-permute-start.15 = (bf16[128,1536]{1,0:T(8,128)(2,1)S(1)}, bf16[128,1536]{1,0:T(8,128)(2,1)S(1)}, u32[]{:S(2)}, u32[]{:S(2)}) collective-permute-start(bf16[128,1536]{1,0:T(8,128)(2,1)S(1)} %collective-permute-done.12), channel_id=1, source_target_pairs={{0,2},{1,15},{2,4},{3,1},{4,6},{5,3},{6,8},{7,5},{8,10},{9,7},{10,... | collective-permute-start | bytes 1179656 | tf_op jit(solution)/shard_map/ppermute | solution.py:30
  33.7 2.6 %collective-permute-start.10 = (bf16[3,128,768]{2,1,0:T(8,128)(2,1)S(1)}, bf16[3,128,768]{2,1,0:T(8,128)(2,1)S(1)}, u32[]{:S(2)}, u32[]{:S(2)}) collective-permute-start(bf16[3,128,768]{2,1,0:T(8,128)(2,1)S(1)} %pad_maximum_fusion.2.near), channel_id=1, source_target_pairs={{0,16},{1,49},{16,32},{17,1},{32,48},{33,17},{48,0},{49,33},{2,18}... | collective-permute-start | bytes 1769480 | tf_op jit(solution)/shard_map/ppermute | solution.py:30
  36.4 2.0 %collective-permute-start.6 = (bf16[128,1536]{1,0:T(8,128)(2,1)S(1)}, bf16[128,1536]{1,0:T(8,128)(2,1)S(1)}, u32[]{:S(2)}, u32[]{:S(2)}) collective-permute-start(bf16[128,1536]{1,0:T(8,128)(2,1)S(1)} %collective-permute-done.5), channel_id=1, source_target_pairs={{0,2},{1,15},{2,4},{3,1},{4,6},{5,3},{6,8},{7,5},{8,10},{9,7},{10,... | collective-permute-start | bytes 1179656 | tf_op jit(solution)/shard_map/ppermute | solution.py:30
  41.2 1.9 %collective-permute-done.10.far = bf16[3,128,768]{2,1,0:T(8,128)(2,1)S(1)} collective-permute-done((bf16[3,128,768]{2,1,0:T(8,128)(2,1)S(1)}, bf16[3,128,768]{2,1,0:T(8,128)(2,1)S(1)}, u32[]{:S(2)}, u32[]{:S(2)}) %collective-permute-start.10) | collective-permute-done | bytes 589856 | tf_op jit(solution)/shard_map/ppermute | solution.py:30
  43.5 3.0 %collective-permute-start.11 = (bf16[128,1536]{1,0:T(8,128)(2,1)S(1)}, bf16[128,1536]{1,0:T(8,128)(2,1)S(1)}, u32[]{:S(2)}, u32[]{:S(2)}) collective-permute-start(bf16[128,1536]{1,0:T(8,128)(2,1)S(1)} %collective-permute-done.6), channel_id=1, source_target_pairs={{0,2},{1,15},{2,4},{3,1},{4,6},{5,3},{6,8},{7,5},{8,10},{9,7},{10,... | collective-permute-start | bytes 1179656 | tf_op jit(solution)/shard_map/ppermute | solution.py:30
  47.6 1.4 %fusion.7 = f32[1536,768]{1,0:T(8,128)S(1)} fusion(bf16[512,1536]{1,0:T(8,128)(2,1)S(1)} %pad_maximum_fusion.1, bf16[1024,768]{1,0:T(8,128)(2,1)S(1)} %shard_map.67), kind=kOutput, calls=%fused_computation.17 | convolution fusion | flops 1207959552 | bytes 7077888 | tf_op jit(solution)/shard_map/dot_general | solution.py:184
  49.3 1.4 %fusion.9 = f32[1536,768]{1,0:T(8,128)S(1)} fusion(bf16[512,1536]{1,0:T(8,128)(2,1)S(1)} %pad_maximum_fusion, bf16[1024,768]{1,0:T(8,128)(2,1)S(1)} %shard_map.67), kind=kOutput, calls=%fused_computation.19 | convolution fusion | flops 1207959552 | bytes 7077888 | tf_op jit(solution)/shard_map/dot_general | solution.py:184
  50.8 2.5 %maximum_maximum_fusion.1 = (bf16[512,1536]{1,0:T(8,128)(2,1)S(1)}, bf16[512,1536]{1,0:T(8,128)(2,1)S(1)}) fusion(bf16[128,1536]{1,0:T(8,128)(2,1)S(1)} %collective-permute-done.20, bf16[128,1536]{1,0:T(8,128)(2,1)S(1)} %collective-permute-done.17, bf16[128,1536]{1,0:T(8,128)(2,1)S(1)} %collective-permute-done.19, bf16[512]{0:T(512)(128)(2,1)S(1)} %pad.11.clone, ...), kind=kLoop, calls=%fused_computation.9 | loop fusion | flops 11796480 | bytes 5506048 | tf_op jit(solution)/shard_map/concatenate | solution.py:194
  53.8 1.5 %fusion.4.grad0 = f32[1536,768]{1,0:T(8,128)S(1)} fusion(f32[1536,768]{1,0:T(8,128)S(1)} %fusion.9, bf16[512,1536]{1,0:T(8,128)(2,1)S(1)} %constant_dynamic-update-slice_fusion.5, bf16[1024,768]{1,0:T(8,128)(2,1)S(1)} %shard_map.67), kind=kOutput, calls=%fused_computation.16 | convolution fusion | flops 1209139200 | bytes 11796480 | tf_op jit(solution)/shard_map/dot_general | solution.py:184
  55.3 1.4 %fusion = f32[1536,768]{1,0:T(8,128)S(1)} fusion(bf16[512,1536]{1,0:T(8,128)(2,1)S(1)} %constant_dynamic-update-slice_fusion.4, bf16[1024,768]{1,0:T(8,128)(2,1)S(1)} %shard_map.67), kind=kOutput, calls=%fused_computation.12 | convolution fusion | flops 1207959552 | bytes 7077888 | tf_op jit(solution)/shard_map/dot_general | solution.py:184
  58.5 1.9 %collective-permute-start.24 = (f32[768]{0:T(1024)S(1)}, f32[768]{0:T(1024)S(1)}, u32[]{:S(2)}, u32[]{:S(2)}) collective-permute-start(f32[768]{0:T(1024)S(1)} %add.96), channel_id=1, source_target_pairs={{0,48},{16,0},{32,16},{48,32},{1,49},{17,1},{33,17},{49,33},{2,50}... | collective-permute-start | bytes 9224 | tf_op jit(solution)/shard_map/ppermute | solution.py:20
  60.4 1.4 %collective-permute-start.22 = (f32[768]{0:T(1024)S(1)}, f32[768]{0:T(1024)S(1)}, u32[]{:S(2)}, u32[]{:S(2)}) collective-permute-start(f32[768]{0:T(1024)S(1)} %add.96), channel_id=1, source_target_pairs={{0,32},{16,48},{32,0},{48,16},{1,33},{17,49},{33,1},{49,17},{2,34}... | collective-permute-start | bytes 9224 | tf_op jit(solution)/shard_map/ppermute | solution.py:20
  61.8 2.2 %collective-permute-done.23 = f32[768]{0:T(1024)S(1)} collective-permute-done((f32[768]{0:T(1024)S(1)}, f32[768]{0:T(1024)S(1)}, u32[]{:S(2)}, u32[]{:S(2)}) %collective-permute-start.23) | collective-permute-done | bytes 3104 | tf_op jit(solution)/shard_map/ppermute | solution.py:20
  66.0 1.9 %collective-permute-start.25 = (f32[48,128]{1,0:T(8,128)S(1)}, f32[48,128]{1,0:T(8,128)S(1)}, u32[]{:S(2)}, u32[]{:S(2)}) collective-permute-start(f32[48,128]{1,0:T(8,128)S(1)} %pad_maximum_fusion.4), channel_id=1, source_target_pairs={{0,1},{1,0},{2,3},{3,2},{4,5},{5,4},{6,7},{7,6},{8,9},{9,8},{10,11... | collective-permute-start | bytes 73736 | tf_op jit(solution)/shard_map/ppermute | solution.py:20
  68.8 2.5 %collective-permute-start.27 = (f32[48,128]{1,0:T(8,128)S(1)}, f32[48,128]{1,0:T(8,128)S(1)}, u32[]{:S(2)}, u32[]{:S(2)}) collective-permute-start(f32[48,128]{1,0:T(8,128)S(1)} %fusion.18), channel_id=1, source_target_pairs={{0,64},{1,193},{64,128},{65,1},{128,192},{129,65},{192,0},{193,129... | collective-permute-start | bytes 73736 | tf_op jit(solution)/shard_map/ppermute | solution.py:30
  72.2 2.0 %collective-permute-start.28 = (f32[48,128]{1,0:T(8,128)S(1)}, f32[48,128]{1,0:T(8,128)S(1)}, u32[]{:S(2)}, u32[]{:S(2)}) collective-permute-start(f32[48,128]{1,0:T(8,128)S(1)} %collective-permute-done.27), channel_id=1, source_target_pairs={{0,1},{1,0},{2,3},{3,2},{4,5},{5,4},{6,7},{7,6},{8,9},{9,8},{10,11... | collective-permute-start | bytes 73736 | tf_op jit(solution)/shard_map/ppermute | solution.py:20
  74.2 1.6 %collective-permute-done.26 = f32[48,128]{1,0:T(8,128)S(1)} collective-permute-done((f32[48,128]{1,0:T(8,128)S(1)}, f32[48,128]{1,0:T(8,128)S(1)}, u32[]{:S(2)}, u32[]{:S(2)}) %collective-permute-start.26) | collective-permute-done | bytes 24608 | tf_op jit(solution)/shard_map/ppermute | solution.py:20
  76.0 2.7 %collective-permute-done.29 = f32[48,128]{1,0:T(8,128)S(1)} collective-permute-done((f32[48,128]{1,0:T(8,128)S(1)}, f32[48,128]{1,0:T(8,128)S(1)}, u32[]{:S(2)}, u32[]{:S(2)}) %collective-permute-start.29) | collective-permute-done | bytes 24608 | tf_op jit(solution)/shard_map/ppermute | solution.py:38
  78.6 1.6 %collective-permute-start.31 = (f32[48,128]{1,0:T(8,128)S(1)}, f32[48,128]{1,0:T(8,128)S(1)}, u32[]{:S(2)}, u32[]{:S(2)}) collective-permute-start(f32[48,128]{1,0:T(8,128)S(1)} %add.105.p0), channel_id=1, source_target_pairs={{0,4},{1,13},{2,6},{3,15},{4,8},{5,1},{6,10},{7,3},{8,12},{9,5},{1... | collective-permute-start | bytes 73736 | tf_op jit(solution)/shard_map/ppermute | solution.py:30
  80.2 2.6 %collective-permute-start.30 = (f32[48,128]{1,0:T(8,128)S(1)}, f32[48,128]{1,0:T(8,128)S(1)}, u32[]{:S(2)}, u32[]{:S(2)}) collective-permute-start(f32[48,128]{1,0:T(8,128)S(1)} %add.105.p0), channel_id=1, source_target_pairs={{0,8},{2,10},{4,12},{6,14},{8,0},{10,2},{12,4},{14,6},{1,9},{3,11}... | collective-permute-start | bytes 73736 | tf_op jit(solution)/shard_map/ppermute | solution.py:20
  82.8 3.6 %collective-permute-start.32 = (f32[48,128]{1,0:T(8,128)S(1)}, f32[48,128]{1,0:T(8,128)S(1)}, u32[]{:S(2)}, u32[]{:S(2)}) collective-permute-start(f32[48,128]{1,0:T(8,128)S(1)} %collective-permute-done.31.p2), channel_id=1, source_target_pairs={{0,1},{1,0},{2,3},{3,2},{4,5},{5,4},{6,7},{7,6},{8,9},{9,8},{10,11... | collective-permute-start | bytes 73736 | tf_op jit(solution)/shard_map/ppermute | solution.py:20
  87.9 2.6 %collective-permute-start.34 = (f32[2,128]{1,0:T(2,128)S(1)}, f32[2,128]{1,0:T(2,128)S(1)}, u32[]{:S(2)}, u32[]{:S(2)}) collective-permute-start(f32[2,128]{1,0:T(2,128)S(1)} %get-tuple-element.28.p0), channel_id=1, source_target_pairs={{0,16},{1,49},{16,32},{17,1},{32,48},{33,17},{48,0},{49,33},{2,18}... | collective-permute-start | bytes 3080 | tf_op jit(solution)/shard_map/ppermute | solution.py:30
  91.2 3.1 %collective-permute-start.35 = (f32[2,128]{1,0:T(2,128)S(1)}, f32[2,128]{1,0:T(2,128)S(1)}, u32[]{:S(2)}, u32[]{:S(2)}) collective-permute-start(f32[2,128]{1,0:T(2,128)S(1)} %collective-permute-done.34.p2), channel_id=1, source_target_pairs={{0,1},{1,0},{2,3},{3,2},{4,5},{5,4},{6,7},{7,6},{8,9},{9,8},{10,11... | collective-permute-start | bytes 3080 | tf_op jit(solution)/shard_map/ppermute | solution.py:20
  95.1 3.9 %shard_map.69 = f32[3072,768]{1,0:T(8,128)} custom-call(s32[1]{0:T(128)} %bitcast.core, f32[2,128]{1,0:T(2,128)S(1)} %get-tuple-element.28.p0, f32[2,128]{1,0:T(2,128)S(1)} %collective-permute-done.33.p1, f32[2,128]{1,0:T(2,128)S(1)} %collective-permute-done.34.p2, f32[2,128]{1,0:T(2,128)S(1)} %collective-permute-done.35.p3, ...), custom_call_target="tpu_custom_call" | custom-call | tf_op jit(solution)/shard_map/pallas_call | solution.py:141
  (82 shorter events, 22.7 us)
Async XLA Ops:
  0.6 10.7 %collective-permute-start.1 = (bf16[16,3072]{1,0:T(8,128)(2,1)}, bf16[16,3072]{1,0:T(8,128)(2,1)S(1)}, u32[]{:S(2)}, u32[]{:S(2)}) collective-permute-start(bf16[16,3072]{1,0:T(8,128)(2,1)} %param.4), channel_id=1, source_target_pairs={{0,128},{64,192},{128,0},{192,64},{1,129},{65,193},{129,1},{193,65... | collective-permute-start | bytes 294920 | tf_op jit(solution)/shard_map/ppermute | solution.py:20
  4.5 6.9 %collective-permute-start = (bf16[16,3072]{1,0:T(8,128)(2,1)}, bf16[16,3072]{1,0:T(8,128)(2,1)S(1)}, u32[]{:S(2)}, u32[]{:S(2)}) collective-permute-start(bf16[16,3072]{1,0:T(8,128)(2,1)} %param.4), channel_id=1, source_target_pairs={{0,64},{64,128},{128,192},{192,0},{1,65},{65,129},{129,193},{193,1... | collective-permute-start | bytes 294920 | tf_op jit(solution)/shard_map/ppermute | solution.py:20
  4.9 6.5 %collective-permute-start.2 = (bf16[16,3072]{1,0:T(8,128)(2,1)}, bf16[16,3072]{1,0:T(8,128)(2,1)S(1)}, u32[]{:S(2)}, u32[]{:S(2)}) collective-permute-start(bf16[16,3072]{1,0:T(8,128)(2,1)} %param.4), channel_id=1, source_target_pairs={{0,192},{64,0},{128,64},{192,128},{1,193},{65,1},{129,65},{193,129... | collective-permute-start | bytes 294920 | tf_op jit(solution)/shard_map/ppermute | solution.py:20
  13.8 10.6 %collective-permute-start.4 = (bf16[128,1536]{1,0:T(8,128)(2,1)S(1)}, bf16[128,1536]{1,0:T(8,128)(2,1)S(1)}, u32[]{:S(2)}, u32[]{:S(2)}) collective-permute-start(bf16[128,1536]{1,0:T(8,128)(2,1)S(1)} %get-tuple-element.43), channel_id=1, source_target_pairs={{0,2},{1,15},{2,4},{3,1},{4,6},{5,3},{6,8},{7,5},{8,10},{9,7},{10,... | collective-permute-start | bytes 1179656 | tf_op jit(solution)/shard_map/ppermute | solution.py:30
  18.8 8.9 %collective-permute-start.12 = (bf16[128,1536]{1,0:T(8,128)(2,1)S(1)}, bf16[128,1536]{1,0:T(8,128)(2,1)S(1)}, u32[]{:S(2)}, u32[]{:S(2)}) collective-permute-start(bf16[128,1536]{1,0:T(8,128)(2,1)S(1)} %get-tuple-element.42), channel_id=1, source_target_pairs={{0,2},{1,15},{2,4},{3,1},{4,6},{5,3},{6,8},{7,5},{8,10},{9,7},{10,... | collective-permute-start | bytes 1179656 | tf_op jit(solution)/shard_map/ppermute | solution.py:30
  20.4 9.1 %collective-permute-start.7 = (bf16[128,768]{1,0:T(8,128)(2,1)}, bf16[128,768]{1,0:T(8,128)(2,1)}, u32[]{:S(2)}, u32[]{:S(2)}) collective-permute-start(bf16[128,768]{1,0:T(8,128)(2,1)} %get-tuple-element.39), channel_id=1, source_target_pairs={{0,64},{64,128},{128,192},{192,0},{1,65},{65,129},{129,193},{193,1... | collective-permute-start | bytes 589832 | tf_op jit(solution)/shard_map/ppermute | solution.py:20
  21.0 10.4 %collective-permute-start.9 = (bf16[128,768]{1,0:T(8,128)(2,1)}, bf16[128,768]{1,0:T(8,128)(2,1)}, u32[]{:S(2)}, u32[]{:S(2)}) collective-permute-start(bf16[128,768]{1,0:T(8,128)(2,1)} %get-tuple-element.40), channel_id=1, source_target_pairs={{0,192},{64,0},{128,64},{192,128},{1,193},{65,1},{129,65},{193,129... | collective-permute-start | bytes 589832 | tf_op jit(solution)/shard_map/ppermute | solution.py:20
  23.3 9.2 %collective-permute-start.8 = (bf16[128,768]{1,0:T(8,128)(2,1)}, bf16[128,768]{1,0:T(8,128)(2,1)}, u32[]{:S(2)}, u32[]{:S(2)}) collective-permute-start(bf16[128,768]{1,0:T(8,128)(2,1)} %get-tuple-element.41), channel_id=1, source_target_pairs={{0,128},{64,192},{128,0},{192,64},{1,129},{65,193},{129,1},{193,65... | collective-permute-start | bytes 589832 | tf_op jit(solution)/shard_map/ppermute | solution.py:20
  24.5 11.9 %collective-permute-start.5 = (bf16[128,1536]{1,0:T(8,128)(2,1)S(1)}, bf16[128,1536]{1,0:T(8,128)(2,1)S(1)}, u32[]{:S(2)}, u32[]{:S(2)}) collective-permute-start(bf16[128,1536]{1,0:T(8,128)(2,1)S(1)} %collective-permute-done.4), channel_id=1, source_target_pairs={{0,2},{1,15},{2,4},{3,1},{4,6},{5,3},{6,8},{7,5},{8,10},{9,7},{10,... | collective-permute-start | bytes 1179656 | tf_op jit(solution)/shard_map/ppermute | solution.py:30
  27.7 10.6 %collective-permute-start.13 = (bf16[128,1536]{1,0:T(8,128)(2,1)S(1)}, bf16[128,1536]{1,0:T(8,128)(2,1)}, u32[]{:S(2)}, u32[]{:S(2)}) collective-permute-start(bf16[128,1536]{1,0:T(8,128)(2,1)S(1)} %collective-permute-done.12), channel_id=1, source_target_pairs={{0,1},{1,0},{2,3},{3,2},{4,5},{5,4},{6,7},{7,6},{8,9},{9,8},{10,11... | collective-permute-start | bytes 1179656 | tf_op jit(solution)/shard_map/ppermute | solution.py:20
  29.5 10.0 %collective-permute-start.15 = (bf16[128,1536]{1,0:T(8,128)(2,1)S(1)}, bf16[128,1536]{1,0:T(8,128)(2,1)S(1)}, u32[]{:S(2)}, u32[]{:S(2)}) collective-permute-start(bf16[128,1536]{1,0:T(8,128)(2,1)S(1)} %collective-permute-done.12), channel_id=1, source_target_pairs={{0,2},{1,15},{2,4},{3,1},{4,6},{5,3},{6,8},{7,5},{8,10},{9,7},{10,... | collective-permute-start | bytes 1179656 | tf_op jit(solution)/shard_map/ppermute | solution.py:30
  31.4 8.1 %collective-permute-start.14 = (bf16[128,1536]{1,0:T(8,128)(2,1)S(1)}, bf16[128,1536]{1,0:T(8,128)(2,1)S(1)}, u32[]{:S(2)}, u32[]{:S(2)}) collective-permute-start(bf16[128,1536]{1,0:T(8,128)(2,1)S(1)} %collective-permute-done.4), channel_id=1, source_target_pairs={{0,1},{1,0},{2,3},{3,2},{4,5},{5,4},{6,7},{7,6},{8,9},{9,8},{10,11... | collective-permute-start | bytes 1179656 | tf_op jit(solution)/shard_map/ppermute | solution.py:20
  33.7 9.4 %collective-permute-start.10 = (bf16[3,128,768]{2,1,0:T(8,128)(2,1)S(1)}, bf16[3,128,768]{2,1,0:T(8,128)(2,1)S(1)}, u32[]{:S(2)}, u32[]{:S(2)}) collective-permute-start(bf16[3,128,768]{2,1,0:T(8,128)(2,1)S(1)} %pad_maximum_fusion.2.near), channel_id=1, source_target_pairs={{0,16},{1,49},{16,32},{17,1},{32,48},{33,17},{48,0},{49,33},{2,18}... | collective-permute-start | bytes 1769480 | tf_op jit(solution)/shard_map/ppermute | solution.py:30
  36.4 7.2 %collective-permute-start.6 = (bf16[128,1536]{1,0:T(8,128)(2,1)S(1)}, bf16[128,1536]{1,0:T(8,128)(2,1)S(1)}, u32[]{:S(2)}, u32[]{:S(2)}) collective-permute-start(bf16[128,1536]{1,0:T(8,128)(2,1)S(1)} %collective-permute-done.5), channel_id=1, source_target_pairs={{0,2},{1,15},{2,4},{3,1},{4,6},{5,3},{6,8},{7,5},{8,10},{9,7},{10,... | collective-permute-start | bytes 1179656 | tf_op jit(solution)/shard_map/ppermute | solution.py:30
  39.6 9.4 %collective-permute-start.17 = (bf16[128,1536]{1,0:T(8,128)(2,1)S(1)}, bf16[128,1536]{1,0:T(8,128)(2,1)S(1)}, u32[]{:S(2)}, u32[]{:S(2)}) collective-permute-start(bf16[128,1536]{1,0:T(8,128)(2,1)S(1)} %collective-permute-done.15), channel_id=1, source_target_pairs={{0,2},{1,15},{2,4},{3,1},{4,6},{5,3},{6,8},{7,5},{8,10},{9,7},{10,... | collective-permute-start | bytes 1179656 | tf_op jit(solution)/shard_map/ppermute | solution.py:30
  40.7 10.0 %collective-permute-start.16 = (bf16[128,1536]{1,0:T(8,128)(2,1)S(1)}, bf16[128,1536]{1,0:T(8,128)(2,1)S(1)}, u32[]{:S(2)}, u32[]{:S(2)}) collective-permute-start(bf16[128,1536]{1,0:T(8,128)(2,1)S(1)} %collective-permute-done.15), channel_id=1, source_target_pairs={{0,1},{1,0},{2,3},{3,2},{4,5},{5,4},{6,7},{7,6},{8,9},{9,8},{10,11... | collective-permute-start | bytes 1179656 | tf_op jit(solution)/shard_map/ppermute | solution.py:20
  40.7 10.0 %collective-permute-start.19 = (bf16[128,1536]{1,0:T(8,128)(2,1)S(1)}, bf16[128,1536]{1,0:T(8,128)(2,1)S(1)}, u32[]{:S(2)}, u32[]{:S(2)}) collective-permute-start(bf16[128,1536]{1,0:T(8,128)(2,1)S(1)} %collective-permute-done.5), channel_id=1, source_target_pairs={{0,1},{1,0},{2,3},{3,2},{4,5},{5,4},{6,7},{7,6},{8,9},{9,8},{10,11... | collective-permute-start | bytes 1179656 | tf_op jit(solution)/shard_map/ppermute | solution.py:20
  43.5 9.8 %collective-permute-start.11 = (bf16[128,1536]{1,0:T(8,128)(2,1)S(1)}, bf16[128,1536]{1,0:T(8,128)(2,1)S(1)}, u32[]{:S(2)}, u32[]{:S(2)}) collective-permute-start(bf16[128,1536]{1,0:T(8,128)(2,1)S(1)} %collective-permute-done.6), channel_id=1, source_target_pairs={{0,2},{1,15},{2,4},{3,1},{4,6},{5,3},{6,8},{7,5},{8,10},{9,7},{10,... | collective-permute-start | bytes 1179656 | tf_op jit(solution)/shard_map/ppermute | solution.py:30
  47.2 3.6 %collective-permute-start.20 = (bf16[128,1536]{1,0:T(8,128)(2,1)S(1)}, bf16[128,1536]{1,0:T(8,128)(2,1)S(1)}, u32[]{:S(2)}, u32[]{:S(2)}) collective-permute-start(bf16[128,1536]{1,0:T(8,128)(2,1)S(1)} %collective-permute-done.6), channel_id=1, source_target_pairs={{0,1},{1,0},{2,3},{3,2},{4,5},{5,4},{6,7},{7,6},{8,9},{9,8},{10,11... | collective-permute-start | bytes 1179656 | tf_op jit(solution)/shard_map/ppermute | solution.py:20
  58.5 3.3 %collective-permute-start.24 = (f32[768]{0:T(1024)S(1)}, f32[768]{0:T(1024)S(1)}, u32[]{:S(2)}, u32[]{:S(2)}) collective-permute-start(f32[768]{0:T(1024)S(1)} %add.96), channel_id=1, source_target_pairs={{0,48},{16,0},{32,16},{48,32},{1,49},{17,1},{33,17},{49,33},{2,50}... | collective-permute-start | bytes 9224 | tf_op jit(solution)/shard_map/ppermute | solution.py:20
  60.4 3.7 %collective-permute-start.23 = (f32[768]{0:T(1024)S(1)}, f32[768]{0:T(1024)S(1)}, u32[]{:S(2)}, u32[]{:S(2)}) collective-permute-start(f32[768]{0:T(1024)S(1)} %add.96), channel_id=1, source_target_pairs={{0,16},{16,32},{32,48},{48,0},{1,17},{17,33},{33,49},{49,1},{2,18}... | collective-permute-start | bytes 9224 | tf_op jit(solution)/shard_map/ppermute | solution.py:20
  60.4 4.0 %collective-permute-start.22 = (f32[768]{0:T(1024)S(1)}, f32[768]{0:T(1024)S(1)}, u32[]{:S(2)}, u32[]{:S(2)}) collective-permute-start(f32[768]{0:T(1024)S(1)} %add.96), channel_id=1, source_target_pairs={{0,32},{16,48},{32,0},{48,16},{1,33},{17,49},{33,1},{49,17},{2,34}... | collective-permute-start | bytes 9224 | tf_op jit(solution)/shard_map/ppermute | solution.py:20
  66.0 2.8 %collective-permute-start.25 = (f32[48,128]{1,0:T(8,128)S(1)}, f32[48,128]{1,0:T(8,128)S(1)}, u32[]{:S(2)}, u32[]{:S(2)}) collective-permute-start(f32[48,128]{1,0:T(8,128)S(1)} %pad_maximum_fusion.4), channel_id=1, source_target_pairs={{0,1},{1,0},{2,3},{3,2},{4,5},{5,4},{6,7},{7,6},{8,9},{9,8},{10,11... | collective-permute-start | bytes 73736 | tf_op jit(solution)/shard_map/ppermute | solution.py:20
  68.8 3.4 %collective-permute-start.27 = (f32[48,128]{1,0:T(8,128)S(1)}, f32[48,128]{1,0:T(8,128)S(1)}, u32[]{:S(2)}, u32[]{:S(2)}) collective-permute-start(f32[48,128]{1,0:T(8,128)S(1)} %fusion.18), channel_id=1, source_target_pairs={{0,64},{1,193},{64,128},{65,1},{128,192},{129,65},{192,0},{193,129... | collective-permute-start | bytes 73736 | tf_op jit(solution)/shard_map/ppermute | solution.py:30
  71.2 4.6 %collective-permute-start.26 = (f32[48,128]{1,0:T(8,128)S(1)}, f32[48,128]{1,0:T(8,128)S(1)}, u32[]{:S(2)}, u32[]{:S(2)}) collective-permute-start(f32[48,128]{1,0:T(8,128)S(1)} %fusion.18), channel_id=1, source_target_pairs={{0,128},{64,192},{128,0},{192,64},{1,129},{65,193},{129,1},{193,65... | collective-permute-start | bytes 73736 | tf_op jit(solution)/shard_map/ppermute | solution.py:20
  72.2 3.6 %collective-permute-start.28 = (f32[48,128]{1,0:T(8,128)S(1)}, f32[48,128]{1,0:T(8,128)S(1)}, u32[]{:S(2)}, u32[]{:S(2)}) collective-permute-start(f32[48,128]{1,0:T(8,128)S(1)} %collective-permute-done.27), channel_id=1, source_target_pairs={{0,1},{1,0},{2,3},{3,2},{4,5},{5,4},{6,7},{7,6},{8,9},{9,8},{10,11... | collective-permute-start | bytes 73736 | tf_op jit(solution)/shard_map/ppermute | solution.py:20
  78.6 4.2 %collective-permute-start.31 = (f32[48,128]{1,0:T(8,128)S(1)}, f32[48,128]{1,0:T(8,128)S(1)}, u32[]{:S(2)}, u32[]{:S(2)}) collective-permute-start(f32[48,128]{1,0:T(8,128)S(1)} %add.105.p0), channel_id=1, source_target_pairs={{0,4},{1,13},{2,6},{3,15},{4,8},{5,1},{6,10},{7,3},{8,12},{9,5},{1... | collective-permute-start | bytes 73736 | tf_op jit(solution)/shard_map/ppermute | solution.py:30
  80.2 6.6 %collective-permute-start.30 = (f32[48,128]{1,0:T(8,128)S(1)}, f32[48,128]{1,0:T(8,128)S(1)}, u32[]{:S(2)}, u32[]{:S(2)}) collective-permute-start(f32[48,128]{1,0:T(8,128)S(1)} %add.105.p0), channel_id=1, source_target_pairs={{0,8},{2,10},{4,12},{6,14},{8,0},{10,2},{12,4},{14,6},{1,9},{3,11}... | collective-permute-start | bytes 73736 | tf_op jit(solution)/shard_map/ppermute | solution.py:20
  82.8 4.5 %collective-permute-start.32 = (f32[48,128]{1,0:T(8,128)S(1)}, f32[48,128]{1,0:T(8,128)S(1)}, u32[]{:S(2)}, u32[]{:S(2)}) collective-permute-start(f32[48,128]{1,0:T(8,128)S(1)} %collective-permute-done.31.p2), channel_id=1, source_target_pairs={{0,1},{1,0},{2,3},{3,2},{4,5},{5,4},{6,7},{7,6},{8,9},{9,8},{10,11... | collective-permute-start | bytes 73736 | tf_op jit(solution)/shard_map/ppermute | solution.py:20
  87.9 3.3 %collective-permute-start.34 = (f32[2,128]{1,0:T(2,128)S(1)}, f32[2,128]{1,0:T(2,128)S(1)}, u32[]{:S(2)}, u32[]{:S(2)}) collective-permute-start(f32[2,128]{1,0:T(2,128)S(1)} %get-tuple-element.28.p0), channel_id=1, source_target_pairs={{0,16},{1,49},{16,32},{17,1},{32,48},{33,17},{48,0},{49,33},{2,18}... | collective-permute-start | bytes 3080 | tf_op jit(solution)/shard_map/ppermute | solution.py:30
  90.5 3.9 %collective-permute-start.33 = (f32[2,128]{1,0:T(2,128)S(1)}, f32[2,128]{1,0:T(2,128)S(1)}, u32[]{:S(2)}, u32[]{:S(2)}) collective-permute-start(f32[2,128]{1,0:T(2,128)S(1)} %get-tuple-element.28.p0), channel_id=1, source_target_pairs={{0,32},{16,48},{32,0},{48,16},{1,33},{17,49},{33,1},{49,17},{2,34}... | collective-permute-start | bytes 3080 | tf_op jit(solution)/shard_map/ppermute | solution.py:20
  91.2 3.9 %collective-permute-start.35 = (f32[2,128]{1,0:T(2,128)S(1)}, f32[2,128]{1,0:T(2,128)S(1)}, u32[]{:S(2)}, u32[]{:S(2)}) collective-permute-start(f32[2,128]{1,0:T(2,128)S(1)} %collective-permute-done.34.p2), channel_id=1, source_target_pairs={{0,1},{1,0},{2,3},{3,2},{4,5},{5,4},{6,7},{7,6},{8,9},{9,8},{10,11... | collective-permute-start | bytes 3080 | tf_op jit(solution)/shard_map/ppermute | solution.py:20
  (7 other events, 45.4 us)
